TPU v7x, 128 devices: a whole 4x4x4 slice. The times are simulated.
128 devices in a mesh: grp: 16 (over y_hi, z, core), tp: 8 (over y_lo, x).
Axes of the slice: x: 4, y: 4 (y_hi: 2, y_lo: 2; y = y_hi * 2 + y_lo), z: 4, core: 2. Of those that a mesh axis runs over, the one named last changes fastest.
Arguments:
- tokens: bfloat16 [1024, 4, 8192], P('grp', None, 'tp'), may hold values from -600 to 600
- w_qkv: bfloat16 [8192, 10240], P(('grp', 'tp')), may hold values from -0.0625 to 0.0625
- w_out: bfloat16 [8192, 8192], P(('grp', 'tp')), may hold values from -0.0625 to 0.0625
- kv_cache: bfloat16 [2048, 128, 2, 1024], P('grp', None, None, 'tp'), may hold values from -384 to 384
- row_pages: int32 [16, 64], P('grp'), may hold values from 1 to 16, 128 in all within a row
- last_fill: int32 [16, 64], P('grp'), may hold values from 1 to 128
- page_order: int32 [16, 128], P('grp'), may hold values from 0 to 127, each once within a row
Outputs:
- mixed: bfloat16 [1024, 4, 8192], P('grp', None, 'tp')
Inputs may be any that keep to these rules, and one draw needn't show every extreme that they name: `row_pages`: in each group the counts sum to 128, and one count equals 16. `page_order`: each row is a permutation of the group's pool pages.
All inputs are finite; a program needn't handle non-finite values.
Results may differ from a plain program's by a relative error of at most 0.019.
Values may be sent and summed in bfloat16 or wider, within the bound.
A program may use at most 256 MiB of HBM per device.

v0:
```python
import math

import jax
import jax.numpy as jnp
from jax import lax
from jax.sharding import PartitionSpec as P

HQ = 64
KVH = 8
HD = 128
BLOCK = 128
MAXP = 16


epsilon = 1e-05


def fresh_scores(queries, new_key, score_scale):
    raw_scores = (
        jnp.einsum("rskgd,rukd->rkgsu", queries, new_key, preferred_element_type=jnp.float32)
        * score_scale
    )
    step_count = queries.shape[1]
    causal = jnp.arange(step_count)[:, None] >= jnp.arange(step_count)[None, :]
    return (jnp.where(causal, raw_scores, -jnp.inf), causal)


def slot_attend(queries, new_key, new_value, cache_view, page_table, lengths, score_scale):
    row_count = queries.shape[0]
    row_block = math.gcd(row_count, 32)
    block_count = row_count // row_block

    def split_rows(array):
        return array.reshape((block_count, row_block) + array.shape[1:])

    def attend_block(packed):
        query_blk, key_blk, value_blk, table_blk, length_blk = packed
        gathered = cache_view[table_blk]
        flat_cache = gathered.reshape(row_block, -1, 2, gathered.shape[4], gathered.shape[5])
        cache_scores = (
            jnp.einsum(
                "rskgd,rtkd->rkgst",
                query_blk,
                flat_cache[:, :, 0],
                preferred_element_type=jnp.float32,
            )
            * score_scale
        )
        token_pos = jnp.arange(flat_cache.shape[1], dtype=jnp.int32)
        live_mask = (token_pos[None, :] < length_blk[:, None])[:, None, None, None, :]
        cache_scores = jnp.where(live_mask, cache_scores, -jnp.inf)
        new_scores, causal = fresh_scores(query_blk, key_blk, score_scale)
        row_top = jnp.maximum(jnp.max(cache_scores, axis=-1), jnp.max(new_scores, axis=-1))
        cache_prob = jnp.where(live_mask, jnp.exp(cache_scores - row_top[..., None]), 0.0)
        new_prob = jnp.where(causal, jnp.exp(new_scores - row_top[..., None]), 0.0)
        row_total = jnp.sum(cache_prob, axis=-1) + jnp.sum(new_prob, axis=-1)
        cache_weight = (cache_prob / row_total[..., None]).astype(jnp.bfloat16)
        new_weight = (new_prob / row_total[..., None]).astype(jnp.bfloat16)
        context = jnp.einsum(
            "rkgst,rtkd->rskgd",
            cache_weight,
            flat_cache[:, :, 1],
            preferred_element_type=jnp.float32,
        )
        context = context + jnp.einsum(
            "rkgsu,rukd->rskgd", new_weight, value_blk, preferred_element_type=jnp.float32
        )
        return context.astype(jnp.bfloat16)

    result = lax.map(
        attend_block,
        (
            split_rows(queries),
            split_rows(new_key),
            split_rows(new_value),
            split_rows(page_table),
            split_rows(lengths),
        ),
    )
    return result.reshape((row_count,) + result.shape[2:])


def per_device(tokens, w_qkv, w_out, kv_cache, row_pages, last_fill, page_order):
    tok_rows, step_count, _ = tokens.shape
    gathered = lax.all_gather(tokens, "tp", axis=2, tiled=True)
    full_width = gathered.shape[2]
    widened = gathered.astype(jnp.float32)
    normed = (
        widened * lax.rsqrt(jnp.mean(widened * widened, axis=2, keepdims=True) + epsilon)
    ).astype(jnp.bfloat16)
    flattened = normed.reshape(tok_rows * step_count, full_width)
    qkv_part, out_part = (
        lax.all_to_all(w_qkv, "tp", split_axis=1, concat_axis=0, tiled=True),
        lax.all_to_all(w_out, "tp", split_axis=1, concat_axis=0, tiled=True),
    )
    qkv_block, out_block = (
        lax.all_gather(qkv_part, "grp", axis=0, tiled=True),
        lax.all_gather(out_part, "grp", axis=0, tiled=True),
    )
    projected = jnp.dot(flattened, qkv_block, preferred_element_type=jnp.float32)
    per_group = HQ // KVH
    kv_heads = kv_cache.shape[3] // HD
    qkv_local = projected.astype(jnp.bfloat16).reshape(
        tok_rows, step_count, kv_heads, per_group + 2, HD
    )
    queries = qkv_local[:, :, :, :per_group]
    new_key = qkv_local[:, :, :, per_group]
    new_value = qkv_local[:, :, :, per_group + 1]
    page_counts = row_pages.reshape(-1)
    pool_order = page_order.reshape(-1)
    pool_pages = pool_order.shape[0]
    lengths = (page_counts - 1) * BLOCK + last_fill.reshape(-1)
    row_starts = jnp.cumsum(page_counts) - page_counts
    cache_view = kv_cache.reshape(pool_pages, kv_cache.shape[1], 2, kv_heads, HD)
    score_scale = HD ** (-0.5)
    slot_range = jnp.arange(MAXP, dtype=jnp.int32)
    page_table = pool_order[jnp.minimum(row_starts[:, None] + slot_range[None, :], pool_pages - 1)]
    context = slot_attend(queries, new_key, new_value, cache_view, page_table, lengths, score_scale)
    context_flat = context.reshape(tok_rows * step_count, -1)
    terms = lax.dot_general(
        context_flat, out_block, (((1,), (1,)), ((), ())), preferred_element_type=jnp.float32
    )
    mixed = lax.psum_scatter(terms.astype(jnp.bfloat16), "tp", scatter_dimension=1, tiled=True)
    return mixed.reshape(tok_rows, step_count, -1)


def solution(mesh):
    placed = (
        P("grp", None, "tp"),
        P(("grp", "tp"), None),
        P(("grp", "tp"), None),
        P("grp", None, None, "tp"),
        P("grp", None),
        P("grp", None),
        P("grp", None),
    )
    return jax.shard_map(
        per_device, mesh=mesh, in_specs=placed, out_specs=P("grp", None, "tp"), check_vma=False
    )
```

profile of v0, /device:TPU:12, one launch (start us, length us, event | category | flops | bytes accessed | tf_op | source)
XLA Modules:
  0.0 433.1 jit_solution(13060927770647677829)
XLA Ops:
  8.7 29.2 %all_to_all.38 = bf16[64,8,1280]{2,0,1:T(8,128)(2,1)} all-to-all(bf16[64,8,1280]{2,0,1:T(8,128)(2,1)S(1)} %bitcast.177), channel_id=1, replica_groups=mesh['grp'=16,'tp'=8] {'tp'}, dimensions={1} | all-to-all | bytes 2621440 | tf_op jit(solution)/shard_map/all_to_all | solution.py:93
  39.3 29.1 %all_to_all.39 = bf16[64,8,1024]{2,0,1:T(8,128)(2,1)} all-to-all(bf16[64,8,1024]{2,0,1:T(8,128)(2,1)S(1)} %bitcast.179), channel_id=1, replica_groups=mesh['grp'=16,'tp'=8] {'tp'}, dimensions={1} | all-to-all | bytes 2097152 | tf_op jit(solution)/shard_map/all_to_all | solution.py:94
  69.0 6.6 %gather_fusion.1 = s32[1024]{0:T(1024)S(1)} fusion(s32[128]{0:T(128)S(1)} %bitcast.171, s32[1024]{0:T(1024)S(1)} %broadcast_clamp_fusion), kind=kCustom, calls=%fused_computation.1 | custom fusion | bytes 12288 | tf_op jit(solution)/shard_map/gather | solution.py:117
  75.6 9.2 %copy.84 = bf16[128,128,2,128]{3,1,2,0:T(8,128)(2,1)} copy(bf16[128,128,2,128]{3,2,1,0:T(2,128)(2,1)} %param.12) | data formatting | bytes 16777216 | tf_op args[3]
  84.9 4.4 %fusion.33 = f32[64,4]{1,0:T(8,128)S(1)} fusion(bf16[64,4,8192]{2,1,0:T(4,128)(2,1)} %all-gather.4.cloned.1.call-done), kind=kLoop, calls=%fused_computation.57 | loop fusion | flops 6291200 | bytes 4195328 | tf_op jit(solution)/shard_map/reduce_sum | solution.py:89
  89.3 7.9 %fusion.34 = bf16[64,4,8192]{2,1,0:T(4,128)(2,1)} fusion(bf16[64,4,8192]{2,1,0:T(4,128)(2,1)} %all-gather.4.cloned.1.call-done, f32[64,4]{1,0:T(8,128)S(1)} %add_rsqrt_fusion), kind=kLoop, calls=%fused_computation.58 | loop fusion | flops 6291456 | bytes 8389632 | tf_op jit(solution)/shard_map/convert_element_type | solution.py:90
  97.2 7.0 %reshape.248 = bf16[256,8192]{1,0:T(8,128)(2,1)} reshape(bf16[64,4,8192]{2,1,0:T(4,128)(2,1)} %fusion.34) | data formatting | bytes 8388608 | tf_op jit(solution)/shard_map/reshape | solution.py:91
  104.2 109.0 %all-gather.6.cloned.1.call-done = bf16[8192,1280]{1,0:T(8,128)(2,1)} async-done(((bf16[512,1280]{1,0:T(8,128)(2,1)}), bf16[8192,1280]{1,0:T(8,128)(2,1)}) %all-gather.6.cloned.1.call-update) | async-done | bytes 20971536 | tf_op jit(solution)/shard_map/all_gather | solution.py:97
  213.2 13.4 %convolution_convert_fusion.1 = bf16[256,1280]{1,0:T(8,128)(2,1)S(1)} fusion(bf16[256,8192]{1,0:T(8,128)(2,1)} %reshape.248, bf16[8192,1280]{1,0:T(8,128)(2,1)} %all-gather.6.cloned.1.call-done), kind=kOutput, calls=%fused_computation.60 | convolution fusion | flops 5369036800 | bytes 25821184 | tf_op jit(solution)/shard_map/dot_general | solution.py:100
  227.4 137.9 %while.10 = (s32[]{:T(128)}, bf16[2,32,4,1,8,128]{5,4,2,1,3,0:T(8,128)(2,1)S(1)}, s32[2,32,16]{2,1,0:T(8,128)S(1)}, bf16[128,128,2,1,128]{4,1,3,2,0:T(8,128)(2,1...) while((s32[]{:T(128)}, ...), condition=%wide.region_7.8_spmd, body=%wide.region_2.7_spmd.sunk | while | flops 1105568256 | bytes 229476368 | solution.py:70
  227.7 19.6 %gather_fusion = bf16[512,128,2,128]{3,1,2,0:T(8,128)(2,1)} fusion(bf16[128,128,2,128]{3,1,2,0:T(8,128)(2,1)} %bitcast.173, s32[1024]{0:T(1024)S(1)} %pad_clamp_fusion.2), kind=kCustom, calls=%fused_computation.clone.1 | custom fusion | bytes 67110912 | tf_op jit(solution)/shard_map/while/body/eval_jaxpr/gather | solution.py:38
  247.3 23.8 %copy.92 = bf16[512,128,2,128]{3,1,0,2:T(8,128)(2,1)} copy(bf16[512,128,2,128]{3,1,2,0:T(8,128)(2,1)} %gather_fusion) | data formatting | bytes 67108864 | tf_op jit(solution)/shard_map/while/body/eval_jaxpr/gather | solution.py:38
  271.2 9.4 %bitcast_reduce_fusion.2 = (f32[32,8,4]{1,2,0:T(4,128)S(1)}, f32[32,2048,4,8]{1,3,2,0:T(8,128)S(1)}) fusion(pred[32,2048]{1,0:T(8,128)(4,1)S(1)} %iota_compare_fusion.4, bf16[2,32,4,1,8,128]{5,4,2,1,3,0:T(8,128)(2,1)S(1)} %get-tuple-element.196, s32[]{:T(128)} %get-tuple-element.182, bf16[32,2048,2,1,128]{4,1,0,3,2:T(8,128)(2,1)} %bitcast.174), kind=kOutput, calls=%fused_computation.7.clone.1 | convolution fusion | flops 543161344 | bytes 25498112 | tf_op jit(solution)/shard_map/while/body/eval_jaxpr/rskgd,rtkd->rkgst/dot_general | solution.py:41
  282.2 1.6 copy-done.2
  283.8 2.7 fusion.54
  286.5 10.0 %fusion.56 = f32[32,128,8,4]{1,2,3,0:T(8,128)S(1)} fusion(bf16[32,2048,2,1,128]{4,1,0,3,2:T(8,128)(2,1)} %bitcast.175, f32[32,2048,4,8]{1,3,2,0:T(8,128)} %copy-done.2, f32[32,8,4]{1,2,0:T(4,128)S(1)} %add.119, f32[32,8,4]{1,2,0:T(4,128)S(1)} %max.10, pred[32,2048]{1,0:T(8,128)(4,1)S(1)} %iota_compare_fusion.4), kind=kOutput, calls=%fused_computation.5.clone.1 | convolution fusion | flops 549453824 | bytes 25952256 | tf_op jit(solution)/shard_map/while/body/eval_jaxpr/rkgst,rtkd->rskgd/dot_general | solution.py:59
  297.0 19.6 %gather_fusion = bf16[512,128,2,128]{3,1,2,0:T(8,128)(2,1)} fusion(bf16[128,128,2,128]{3,1,2,0:T(8,128)(2,1)} %bitcast.173, s32[1024]{0:T(1024)S(1)} %pad_clamp_fusion.2), kind=kCustom, calls=%fused_computation.clone.1 | custom fusion | bytes 67110912 | tf_op jit(solution)/shard_map/while/body/eval_jaxpr/gather | solution.py:38
  316.6 23.1 %copy.92 = bf16[512,128,2,128]{3,1,0,2:T(8,128)(2,1)} copy(bf16[512,128,2,128]{3,1,2,0:T(8,128)(2,1)} %gather_fusion) | data formatting | bytes 67108864 | tf_op jit(solution)/shard_map/while/body/eval_jaxpr/gather | solution.py:38
  339.8 9.2 %bitcast_reduce_fusion.2 = (f32[32,8,4]{1,2,0:T(4,128)S(1)}, f32[32,2048,4,8]{1,3,2,0:T(8,128)S(1)}) fusion(pred[32,2048]{1,0:T(8,128)(4,1)S(1)} %iota_compare_fusion.4, bf16[2,32,4,1,8,128]{5,4,2,1,3,0:T(8,128)(2,1)S(1)} %get-tuple-element.196, s32[]{:T(128)} %get-tuple-element.182, bf16[32,2048,2,1,128]{4,1,0,3,2:T(8,128)(2,1)} %bitcast.174), kind=kOutput, calls=%fused_computation.7.clone.1 | convolution fusion | flops 543161344 | bytes 25498112 | tf_op jit(solution)/shard_map/while/body/eval_jaxpr/rskgd,rtkd->rkgst/dot_general | solution.py:41
  352.1 2.7 fusion.54
  354.9 10.0 %fusion.56 = f32[32,128,8,4]{1,2,3,0:T(8,128)S(1)} fusion(bf16[32,2048,2,1,128]{4,1,0,3,2:T(8,128)(2,1)} %bitcast.175, f32[32,2048,4,8]{1,3,2,0:T(8,128)} %copy-done.2, f32[32,8,4]{1,2,0:T(4,128)S(1)} %add.119, f32[32,8,4]{1,2,0:T(4,128)S(1)} %max.10, pred[32,2048]{1,0:T(8,128)(4,1)S(1)} %iota_compare_fusion.4), kind=kOutput, calls=%fused_computation.5.clone.1 | convolution fusion | flops 549453824 | bytes 25952256 | tf_op jit(solution)/shard_map/while/body/eval_jaxpr/rkgst,rtkd->rskgd/dot_general | solution.py:59
  365.3 9.5 %convolution_convert_fusion = bf16[256,8192]{1,0:T(8,128)(2,1)} fusion(bf16[8192,1024]{1,0:T(8,128)(2,1)} %all-gather.8.cloned.1.call-done, bf16[32,8,8,128]{3,2,1,0:T(8,128)(2,1)S(1)} %bitcast.186), kind=kOutput, calls=%fused_computation.56 | convolution fusion | flops 4297064448 | bytes 21495808 | tf_op jit(solution)/shard_map/dot_general | solution.py:120
  374.9 49.7 %reduce-scatter.2.cloned.1.call-done = bf16[256,1024]{1,0:T(8,128)(2,1)} async-done(((bf16[256,8192]{1,0:T(8,128)(2,1)}), bf16[256,1024]{1,0:T(8,128)(2,1)}) %reduce-scatter.2.cloned.1.call-update) | async-done | bytes 524304 | tf_op jit(solution)/shard_map/reduce_scatter | solution.py:123
  424.6 2.0 reshape.251
  (64 shorter events, 11.1 us)
Async XLA Ops:
  6.5 62.4 %copy-start = (s32[1,128]{1,0:T(1,128)S(1)}, s32[1,128]{1,0:T(1,128)}, u32[]{:S(2)}) copy-start(s32[1,128]{1,0:T(1,128)} %param.15) | copy-start | bytes 1540
  6.5 61.9 %copy-start.3 = (s32[1,64]{1,0:T(1,128)S(1)}, s32[1,64]{1,0:T(1,128)}, u32[]{:S(2)}) copy-start(s32[1,64]{1,0:T(1,128)} %param.13) | copy-start | bytes 772
  6.5 78.3 %all-gather.4.cloned.1.call-start = ((), (), s32[]{:S(2)}) async-start(), calls=%async_computation.3 | async-start | bytes 4718592 | tf_op jit(solution)/shard_map/all_gather | solution.py:85
  7.3 206.0 %all-gather.6.cloned.1.call-start = ((), (), s32[]{:S(2)}) async-start(), calls=%async_computation.4 | async-start | bytes 22282240 | tf_op jit(solution)/shard_map/all_gather | solution.py:97
  37.9 327.4 %all-gather.8.cloned.1.call-start = ((), (), s32[]{:S(2)}) async-start(), calls=%async_computation.5 | async-start | bytes 17825792 | tf_op jit(solution)/shard_map/all_gather | solution.py:98
  68.4 356.2 %reduce-scatter.2.cloned.1.call-start = ((), (), s32[]{:S(2)}) async-start(), calls=%async_computation.6 | async-start | bytes 4718592 | tf_op jit(solution)/shard_map/reduce_scatter | solution.py:123
  75.6 9.2 %copy-start.4 = (s32[1,64]{1,0:T(1,128)S(1)}, s32[1,64]{1,0:T(1,128)}, u32[]{:S(2)}) copy-start(s32[1,64]{1,0:T(1,128)} %param.14) | copy-start | bytes 772
  280.6 3.2 copy-start.2
  349.0 3.2 copy-start.2
  365.3 61.3 %copy-start.1 = (s32[1,128]{1,0:T(1,128)S(1)}, s32[1,128]{1,0:T(1,128)}, u32[]{:S(2)}) copy-start(s32[1,128]{1,0:T(1,128)} %param.15) | copy-start | bytes 1540
Sparse Core Ops, SparseCore 0:
  9.0 71.9 all-gather.3
  83.4 129.7 all-gather.5
  215.7 106.8 all-gather.7
  375.0 49.5 reduce-scatter.1
where the time goes:
time: 437 us; the launch traced here: 433 us
  waiting for transfers between devices  159 us (36%)
  local copies, waits for them, and re-layouts  118 us (27%)
  matrix products  64.8 us (15%)
  blocking collectives  58.2 us (13%)
  other arithmetic  19 us (4%)
  between operations  13.3 us (3%)
    all_gather x1, waiting for transfers between devices, per_device(): lax.all_gather(qkv_part, 'grp', axis=0, tiled=True)  109 us
    gather x4, local copies, waits for them, and re-layouts, attend_block(): gathered = cache_view[table_blk]  86 us
    reduce_scatter x1, waiting for transfers between devices, per_device(): lax.psum_scatter(terms.astype(jnp.bfloat16), 'tp', scatter_dimension=1, t...  49.7 us
    all_to_all x1, blocking collectives, per_device(): lax.all_to_all(w_qkv, 'tp', split_axis=1, concat_axis=0, tiled=True)  29.2 us
    all_to_all x1, blocking collectives, per_device(): lax.all_to_all(w_out, 'tp', split_axis=1, concat_axis=0, tiled=True)  29.1 us
    dot_general x2, matrix products, attend_block(): jnp.einsum('rkgst,rtkd->rskgd', cache_weight, flat_cache[:, :, 1], prefer...  19.9 us
    dot_general x2, matrix products, attend_block(): jnp.einsum('rskgd,rtkd->rkgst', query_blk, flat_cache[:, :, 0], preferred...  18.5 us
    dot_general x1, matrix products, per_device(): jnp.dot(flattened, qkv_block, preferred_element_type=jnp.float32)  13.4 us
  transfers between devices with their start and end apart: 4, of which 2 were waited for; matrix products, arithmetic and copies ran while one was open for 43% of the time, Pallas kernels for 0%

commit v1 on v0

v1 whole, which is shorter than its diff:
```python
import functools

import jax
import jax.numpy as jnp
from jax import lax
from jax.experimental import pallas as pl
from jax.experimental.pallas import tpu as pltpu
from jax.sharding import PartitionSpec as P

HD = 128
STEPS = 4
PER_GROUP = 8
BLOCK = 128
ROWS = 64
PAGES = 128
TOK = ROWS * STEPS
D = 8192
TP = 8
QC = 1280
OC = 1024
EPS = 1e-05
SCALE = HD ** (-0.5)
MESH = pl.DeviceIdType.MESH
NEG = -1e30
MIB = 1 << 20


def page_tables(row_pages, last_fill, row_of, valid_of, first_of, last_of):
    def rows(r, end):
        end = end + row_pages[r]
        last_of[r] = end - 1
        return end

    lax.fori_loop(0, ROWS, rows, jnp.int32(0))

    def slots(i, carry):
        r, j = carry
        pages = row_pages[r]
        row_of[i] = r
        first_of[i] = j
        valid_of[i] = jnp.where(j == pages - 1, last_fill[r], BLOCK)
        done = j + 1 == pages
        return (
            jnp.minimum(jnp.where(done, r + 1, r), ROWS - 1),
            jnp.where(done, 0, j + 1),
        )

    lax.fori_loop(0, PAGES, slots, (jnp.int32(0), jnp.int32(0)))


def new_tokens(proj, q_ref, m_new, l_new, o_new):
    def group(g, _):
        base = pl.multiple_of(g * 16, 16)
        heads = [
            proj[pl.ds(base, 16), pl.ds(a * HD, HD)].astype(jnp.float32)
            for a in range(PER_GROUP)
        ]
        for r in range(4):
            q_ref[g * 4 + r] = jnp.concatenate(
                [h[4 * r : 4 * r + 4] for h in heads], axis=0
            ).astype(jnp.bfloat16)
        key = proj[pl.ds(base, 16), pl.ds(PER_GROUP * HD, HD)]
        value = proj[pl.ds(base, 16), pl.ds((PER_GROUP + 1) * HD, HD)]
        q = q_ref[pl.ds(g * 4, 4)].reshape(128, HD)
        s = (
            lax.dot_general(
                q, key, (((1,), (1,)), ((), ())), preferred_element_type=jnp.float32
            )
            * SCALE
        )
        i = lax.broadcasted_iota(jnp.int32, s.shape, 0)
        j = lax.broadcasted_iota(jnp.int32, s.shape, 1)
        live = ((i >> 5) == (j >> 2)) & ((j & 3) <= (i & 3))
        s = jnp.where(live, s, -jnp.inf)
        m = jnp.max(s, axis=1, keepdims=True)
        p = jnp.exp(s - m)
        total = jnp.sum(p, axis=1, keepdims=True)
        o = jnp.dot(p.astype(jnp.bfloat16), value, preferred_element_type=jnp.float32)
        m_new[pl.ds(g * 4, 4)] = jnp.broadcast_to(m, (128, HD)).reshape(4, 32, HD)
        l_new[pl.ds(g * 4, 4)] = jnp.broadcast_to(total, (128, HD)).reshape(4, 32, HD)
        o_new[pl.ds(g * 4, 4)] = o.reshape(4, 32, HD)
        return 0

    lax.fori_loop(0, ROWS // 4, group, 0)


def cached_tokens(order, cache, q_ref, row_of, valid_of, m_pg, l_pg, o_pg):
    lane = lax.broadcasted_iota(jnp.int32, (32, 2 * BLOCK), 1)
    even = (lane & 1) == 0

    def some(n, _):
        for k in range(8):
            i = n * 8 + k
            kv = cache[order[i]]
            q = q_ref[row_of[i]]
            s = (
                lax.dot_general(
                    q, kv, (((1,), (1,)), ((), ())), preferred_element_type=jnp.float32
                )
                * SCALE
            )
            s = jnp.where(even & (lane < 2 * valid_of[i]), s, -jnp.inf)
            m = jnp.max(s, axis=1, keepdims=True)
            p = jnp.exp(s - m)
            total = jnp.sum(p, axis=1, keepdims=True)
            w = pltpu.roll(p, 1, 1).astype(jnp.bfloat16)
            o_pg[i] = jnp.dot(w, kv, preferred_element_type=jnp.float32)
            m_pg[i] = jnp.broadcast_to(m, (32, HD))
            l_pg[i] = jnp.broadcast_to(total, (32, HD))
        return 0

    lax.fori_loop(0, PAGES // 8, some, 0)


def join_pages(row_of, first_of, last_of, new, pg, ctx):
    m_new, l_new, o_new = new
    m_pg, l_pg, o_pg = pg

    def slot(i, run):
        r = row_of[i]
        first = first_of[i] == 0
        m0 = jnp.where(first, m_new[r], run[0])
        l0 = jnp.where(first, l_new[r], run[1])
        o0 = jnp.where(first, o_new[r], run[2])
        m1 = m_pg[i]
        m = jnp.maximum(m0, m1)
        a0 = jnp.exp(m0 - m)
        a1 = jnp.exp(m1 - m)
        total = l0 * a0 + l_pg[i] * a1
        o = o0 * a0 + o_pg[i] * a1
        l_pg[i] = total
        o_pg[i] = o
        return m, total, o

    zero = jnp.zeros((32, HD), jnp.float32)
    lax.fori_loop(0, PAGES, slot, (zero, zero, zero))

    def group(g, _):
        rows = []
        for r in range(4):
            i = last_of[g * 4 + r]
            rows.append(o_pg[i] / l_pg[i])
        for a in range(PER_GROUP):
            ctx[pl.ds(pl.multiple_of(g * 16, 16), 16), pl.ds(a * HD, HD)] = jnp.concatenate(
                [o[4 * a : 4 * a + 4] for o in rows], axis=0
            ).astype(jnp.bfloat16)
        return 0

    lax.fori_loop(0, ROWS // 4, group, 0)


def attention_kernel(
    row_pages, last_fill, order, proj, cache_hbm, ctx,
    cache, q_ref, m_new, l_new, o_new, m_pg, l_pg, o_pg,
    row_of, valid_of, first_of, last_of, sems,
):
    def part(n):
        rows = pl.ds(n * 16, 16)
        return pltpu.make_async_copy(cache_hbm.at[rows], cache.at[rows], sems.at[n])

    for n in range(8):
        part(n).start()
    page_tables(row_pages, last_fill, row_of, valid_of, first_of, last_of)
    new_tokens(proj, q_ref, m_new, l_new, o_new)
    for n in range(8):
        part(n).wait()
    cached_tokens(order, cache, q_ref, row_of, valid_of, m_pg, l_pg, o_pg)
    join_pages(row_of, first_of, last_of, (m_new, l_new, o_new), (m_pg, l_pg, o_pg), ctx)


def attention_scratch():
    f32 = jnp.float32
    return [
        pltpu.VMEM((PAGES, 2 * BLOCK, HD), jnp.bfloat16),
        pltpu.VMEM((ROWS, 32, HD), jnp.bfloat16),
        pltpu.VMEM((ROWS, 32, HD), f32),
        pltpu.VMEM((ROWS, 32, HD), f32),
        pltpu.VMEM((ROWS, 32, HD), f32),
        pltpu.VMEM((PAGES, 32, HD), f32),
        pltpu.VMEM((PAGES, 32, HD), f32),
        pltpu.VMEM((PAGES, 32, HD), f32),
        pltpu.SMEM((PAGES,), jnp.int32),
        pltpu.SMEM((PAGES,), jnp.int32),
        pltpu.SMEM((PAGES,), jnp.int32),
        pltpu.SMEM((ROWS,), jnp.int32),
    ]


def attention(row_pages, last_fill, order, proj, cache):
    smem = pl.BlockSpec(memory_space=pltpu.SMEM)
    return pl.pallas_call(
        attention_kernel,
        out_shape=jax.ShapeDtypeStruct((TOK, OC), jnp.bfloat16),
        in_specs=[smem, smem, smem, pl.BlockSpec(memory_space=pltpu.VMEM), pl.BlockSpec(memory_space=pl.ANY)],
        out_specs=pl.BlockSpec(memory_space=pltpu.VMEM),
        scratch_shapes=attention_scratch() + [pltpu.SemaphoreType.DMA((8,))],
        compiler_params=pltpu.CompilerParams(vmem_limit_bytes=40 * MIB),
        name="attention",
    )(row_pages, last_fill, order, proj, cache)


class Place:
    def __init__(self):
        g, t = lax.axis_index("grp"), lax.axis_index("tp")
        self.g, self.t = g, t
        self.core = g % 2
        self.z = (g // 2) % 4
        self.yh = g // 8
        self.yl = t // 4
        self.x = t % 4
        self.s = self.yh * TP + t
        self.zm = (self.z + 3) % 4
        self.zp = (self.z + 1) % 4
        self.z2 = (self.z + 2) % 4

    def grp(self, yh, z, core):
        return (yh * 4 + z) * 2 + core

    def plane(self, k):
        s = (self.s + k) % 16
        return self.grp(s // TP, self.z, self.core), s % TP

    def above(self):
        return self.grp(self.yh, self.zp, self.core), self.t

    def below(self):
        return self.grp(self.yh, self.zm, self.core), self.t

    def other(self):
        return self.grp(self.yh, self.z, 1 - self.core), self.t


def greet(me, extra):
    barrier = pltpu.get_barrier_semaphore()

    def one(k, _):
        pl.semaphore_signal(barrier, inc=1, device_id=me.plane(k), device_id_type=MESH)
        return 0

    lax.fori_loop(1, 16, one, 0)
    for who in extra:
        pl.semaphore_signal(barrier, inc=1, device_id=who, device_id_type=MESH)
    pl.semaphore_wait(barrier, 15 + len(extra))


class Weights:
    def __init__(self, me, w, buf, width, own, sent, up, down, got):
        self.me, self.w, self.buf, self.width = me, w, buf, width
        self.own_sem, self.sent, self.up, self.down, self.got = own, sent, up, down, got

    def columns(self, t):
        return self.w.at[:, pl.ds(pl.multiple_of(t * self.width, self.width), self.width)]

    def own(self):
        me = self.me
        return pltpu.make_async_copy(self.columns(me.t), self.buf.at[me.z, me.s], self.own_sem.at[0])

    def to_plane(self, k):
        me = self.me
        who = me.plane(k)
        return pltpu.make_async_remote_copy(
            self.columns(who[1]), self.buf.at[me.z, me.s],
            self.sent.at[k], self.got.at[me.z, me.s],
            device_id=who, device_id_type=MESH,
        )

    def along(self, z, s, who, sem):
        slot = self.buf.at[z, s]
        return pltpu.make_async_remote_copy(
            slot, slot, sem, self.got.at[z, s], device_id=who, device_id_type=MESH
        )

    def send_up(self, z, s, k):
        return self.along(z, s, self.me.above(), self.up.at[k])

    def send_down(self, z, s, k):
        return self.along(z, s, self.me.below(), self.down.at[k])

    def source(self, k):
        return (self.me.s + 16 - k) % 16

    def start(self):
        def one(k, _):
            self.to_plane(k).start()
            return 0

        self.own().start()
        lax.fori_loop(1, 16, one, 0)

    def pass_own(self):
        me = self.me
        self.own().wait()
        self.send_up(me.z, me.s, 0).start()
        self.send_down(me.z, me.s, 0).start()

        def one(k, _):
            s = self.source(k)
            self.along(me.z, s, me.above(), self.up.at[k]).wait_recv()
            self.send_up(me.z, s, k).start()
            self.send_down(me.z, s, k).start()
            return 0

        lax.fori_loop(1, 16, one, 0)

    def pass_on(self):
        me = self.me

        def got(z, k):
            self.along(z, self.source(k), me.above(), self.up.at[0]).wait_recv()

        def two(n, _):
            k = 2 * n
            got(me.zm, k)
            self.send_up(me.zm, self.source(k), 16 + n).start()
            got(me.zp, k)
            got(me.zp, k + 1)
            self.send_down(me.zp, self.source(k + 1), 16 + n).start()
            got(me.zm, k + 1)
            return 0

        lax.fori_loop(0, 8, two, 0)

    def last(self):
        me = self.me

        def one(k, _):
            self.along(me.z2, self.source(k), me.above(), self.up.at[0]).wait_recv()
            return 0

        lax.fori_loop(0, 16, one, 0)

    def finish(self):
        me = self.me

        def plane(k, _):
            self.to_plane(k).wait_send()
            return 0

        lax.fori_loop(1, 16, plane, 0)

        def ring(k, _):
            self.send_up(me.z, k % 16, k).wait_send()
            self.send_down(me.z, k % 16, k).wait_send()
            return 0

        lax.fori_loop(0, 24, ring, 0)


def weight_sems():
    dma = pltpu.SemaphoreType.DMA
    return [dma((1,)), dma((16,)), dma((24,)), dma((24,)), dma((4, 16))]


def project_kernel(
    tok, w, out,
    xbuf, wbuf, acc, squares, acc_in, squares_in,
    own, sent, up, down, got,
    x_own, x_sent, x_up, x_down, x_got, last_sent, last_got,
):
    me = Place()
    c = me.core
    side = (me.grp(me.yh, me.z, c), (1 - me.yl) * 4 + me.x)
    cross = (me.grp(me.yh, me.z, 1 - c), (1 - me.yl) * 4 + me.x)
    other = me.other()
    right = (me.g, me.yl * 4 + (me.x + 1) % 4)
    left = (me.g, me.yl * 4 + (me.x + 3) % 4)
    greet(me, (me.above(), me.below(), other, cross))

    def half(h):
        return tok.at[:, pl.ds(pl.multiple_of(h * 512, 512), 512)]

    x_own_copy = pltpu.make_async_copy(half(c), xbuf.at[me.t, c], x_own.at[0])
    x_own_copy.start()

    def x_send(n, who, h):
        return pltpu.make_async_remote_copy(
            half(h), xbuf.at[me.t, c], x_sent.at[n], x_got.at[me.t, c],
            device_id=who, device_id_type=MESH,
        )

    firsts = [x_send(0, other, 1 - c), x_send(1, side, c), x_send(2, cross, 1 - c)]
    for copy in firsts:
        copy.start()
    weights = Weights(me, w, wbuf, QC, own, sent, up, down, got)
    weights.start()

    def x_along(t, h, who, sem):
        slot = xbuf.at[t, h]
        return pltpu.make_async_remote_copy(
            slot, slot, sem, x_got.at[t, h], device_id=who, device_id_type=MESH
        )

    t_side = (1 - me.yl) * 4 + me.x
    x_own_copy.wait()
    pieces = [(me.t, c), (me.t, 1 - c), (t_side, c), (t_side, 1 - c)]
    for n, (t, h) in enumerate(pieces):
        if n:
            x_along(t, h, right, x_up.at[0]).wait_recv()
        x_along(t, h, right, x_up.at[n]).start()
        x_along(t, h, left, x_down.at[n]).start()

    weights.pass_own()

    xl, xr, x2 = (me.x + 3) % 4, (me.x + 1) % 4, (me.x + 2) % 4
    for yl in range(2):
        for h in range(2):
            x_along(yl * 4 + xl, h, right, x_up.at[0]).wait_recv()
            x_along(yl * 4 + xr, h, right, x_up.at[0]).wait_recv()
        x_along(yl * 4 + xl, 0, right, x_up.at[4 + yl]).start()
        x_along(yl * 4 + xr, 1, left, x_down.at[4 + yl]).start()

    acc[...] = jnp.zeros_like(acc)
    squares[...] = jnp.zeros_like(squares)

    def multiply(z):
        def tile(n, _):
            cols = pl.ds(pl.multiple_of(n * 256, 256), 256)
            total = acc[:, cols]
            for yh in range(2):
                xs = xbuf[yh * 4 + z].reshape(2 * TOK, 512)
                ws = wbuf[z, pl.ds(yh * 8, 8), :, cols].reshape(512, 256)
                total = total + jnp.dot(xs, ws, preferred_element_type=jnp.float32)
            acc[:, cols] = total
            return 0

        lax.fori_loop(0, QC // 256, tile, 0)

    for yl in range(2):
        for h in range(2):
            x_along(yl * 4 + x2, h, right, x_up.at[0]).wait_recv()

    weights.pass_on()
    multiply(me.z)

    def square(n, _):
        t, r = n // 8, n % 8
        rows = pl.ds(pl.multiple_of((r % 4) * 64, 64), 64)
        v = xbuf[t, r // 4, rows, :].astype(jnp.float32)
        v = v * v
        where = pl.ds(pl.multiple_of(r * 64, 64), 64)
        squares[where, :] += v[:, :128] + v[:, 128:256] + v[:, 256:384] + v[:, 384:]
        return 0

    lax.fori_loop(0, 64, square, 0)
    multiply(me.zm)
    multiply(me.zp)
    weights.last()
    multiply(me.z2)

    mine = pl.ds(pl.multiple_of(c * TOK, TOK), TOK)
    theirs = pl.ds(pl.multiple_of((1 - c) * TOK, TOK), TOK)
    swaps = [
        pltpu.make_async_remote_copy(
            acc.at[theirs], acc_in, last_sent.at[0], last_got.at[0],
            device_id=other, device_id_type=MESH,
        ),
        pltpu.make_async_remote_copy(
            squares.at[theirs], squares_in, last_sent.at[1], last_got.at[1],
            device_id=other, device_id_type=MESH,
        ),
    ]
    for copy in swaps:
        copy.start()
    for copy in firsts:
        copy.wait_send()
    for n in range(6):
        x_along(me.t, c, right, x_up.at[n]).wait_send()
        x_along(me.t, c, left, x_down.at[n]).wait_send()
    weights.finish()
    for copy in swaps:
        copy.wait()
    mean = jnp.sum(squares[mine, :] + squares_in[...], axis=1, keepdims=True) * (1.0 / D)
    gain = lax.rsqrt(mean + EPS)

    def scale(n, _):
        cols = pl.ds(pl.multiple_of(n * 256, 256), 256)
        out[:, cols] = ((acc[mine, cols] + acc_in[:, cols]) * gain).astype(jnp.bfloat16)
        return 0

    lax.fori_loop(0, QC // 256, scale, 0)


def project(tokens, w):
    dma = pltpu.SemaphoreType.DMA
    anywhere = pl.BlockSpec(memory_space=pl.ANY)
    return pl.pallas_call(
        project_kernel,
        out_shape=jax.ShapeDtypeStruct((TOK, QC), jnp.bfloat16),
        in_specs=[anywhere, anywhere],
        out_specs=pl.BlockSpec(memory_space=pltpu.VMEM),
        scratch_shapes=[
            pltpu.VMEM((TP, 2, TOK, 512), jnp.bfloat16),
            pltpu.VMEM((4, 16, 64, QC), jnp.bfloat16),
            pltpu.VMEM((2 * TOK, QC), jnp.float32),
            pltpu.VMEM((2 * TOK, 128), jnp.float32),
            pltpu.VMEM((TOK, QC), jnp.float32),
            pltpu.VMEM((TOK, 128), jnp.float32),
        ]
        + weight_sems()
        + [dma((1,)), dma((3,)), dma((6,)), dma((6,)), dma((TP, 2)), dma((2,)), dma((2,))],
        compiler_params=pltpu.CompilerParams(
            collective_id=0, has_side_effects=True, vmem_limit_bytes=48 * MIB
        ),
        cost_estimate=pl.CostEstimate(
            flops=2 * TOK * D * QC, bytes_accessed=64 * QC * 2, transcendentals=0
        ),
        name="project",
    )(tokens, w)


def output_kernel(
    ctx, w, out,
    cbuf, wbuf, part, terms, edge, edge_in,
    own, sent, up, down, got,
    c_sem, c_got, t_sent, t_got, last_sent, last_got,
):
    me = Place()
    c = me.core
    other = me.other()
    greet(me, (me.above(), me.below(), other))
    weights = Weights(me, w, wbuf, OC, own, sent, up, down, got)
    mine = pltpu.make_async_copy(ctx, cbuf.at[c], c_sem.at[0])
    swap = pltpu.make_async_remote_copy(
        ctx, cbuf.at[c], c_sem.at[1], c_got.at[0], device_id=other, device_id_type=MESH
    )
    mine.start()
    swap.start()
    weights.start()
    weights.pass_own()
    mine.wait()
    swap.wait()

    def give(t):
        return pltpu.make_async_remote_copy(
            part.at[t], terms.at[me.t], t_sent.at[t], t_got.at[me.t],
            device_id=(me.g, t), device_id_type=MESH,
        )

    def multiply(z):
        for yh in range(2):
            t = yh * 4 + z
            xs = cbuf[...].reshape(2 * TOK, OC)

            def tile(n, _, yh=yh, t=t, xs=xs):
                ws = wbuf[z, pl.ds(yh * 8 + n * 4, 4)].reshape(256, OC)
                part[t, :, pl.ds(pl.multiple_of(n * 256, 256), 256)] = lax.dot_general(
                    xs, ws, (((1,), (1,)), ((), ())), preferred_element_type=jnp.float32
                ).astype(jnp.bfloat16)
                return 0

            lax.fori_loop(0, 2, tile, 0)

            @pl.when(t != me.t)
            def _(t=t):
                give(t).start()

    weights.pass_on()
    multiply(me.z)
    multiply(me.zm)
    multiply(me.zp)
    weights.last()
    multiply(me.z2)

    def arrive(k, _):
        t = (me.t + k) % TP
        pltpu.make_async_remote_copy(
            part.at[t], terms.at[t], t_sent.at[t], t_got.at[t],
            device_id=(me.g, t), device_id_type=MESH,
        ).wait()
        return 0

    lax.fori_loop(1, TP, arrive, 0)

    def add(n, _):
        rows = pl.ds(pl.multiple_of(n * 64, 64), 64)
        total = part[me.t, rows, :].astype(jnp.float32)
        for k in range(1, TP):
            total = total + terms[(me.t + k) % TP, rows, :].astype(jnp.float32)
        edge[n // 4, pl.ds(pl.multiple_of((n % 4) * 64, 64), 64), :] = total.astype(jnp.bfloat16)
        return 0

    lax.fori_loop(0, 8, add, 0)
    back = pltpu.make_async_remote_copy(
        edge.at[1 - c], edge_in, last_sent.at[0], last_got.at[0],
        device_id=other, device_id_type=MESH,
    )
    back.start()
    weights.finish()
    out[:, pl.ds(pl.multiple_of(c * 512, 512), 512)] = edge[c]
    back.wait()
    out[:, pl.ds(pl.multiple_of((1 - c) * 512, 512), 512)] = edge_in[...]


def output(ctx, w):
    dma = pltpu.SemaphoreType.DMA
    anywhere = pl.BlockSpec(memory_space=pl.ANY)
    bf16 = jnp.bfloat16
    return pl.pallas_call(
        output_kernel,
        out_shape=jax.ShapeDtypeStruct((TOK, OC), bf16),
        in_specs=[anywhere, anywhere],
        out_specs=pl.BlockSpec(memory_space=pltpu.VMEM),
        scratch_shapes=[
            pltpu.VMEM((2, TOK, OC), bf16),
            pltpu.VMEM((4, 16, 64, OC), bf16),
            pltpu.VMEM((TP, 2 * TOK, 512), bf16),
            pltpu.VMEM((TP, 2 * TOK, 512), bf16),
            pltpu.VMEM((2, TOK, 512), bf16),
            pltpu.VMEM((TOK, 512), bf16),
        ]
        + weight_sems()
        + [dma((2,)), dma((1,)), dma((TP,)), dma((TP,)), dma((1,)), dma((1,))],
        compiler_params=pltpu.CompilerParams(
            collective_id=1, has_side_effects=True, vmem_limit_bytes=48 * MIB
        ),
        cost_estimate=pl.CostEstimate(
            flops=2 * TOK * D * OC, bytes_accessed=64 * OC * 2, transcendentals=0
        ),
        name="output",
    )(ctx, w)


def per_device(tokens, w_qkv, w_out, kv_cache, row_pages, last_fill, page_order):
    projected = project(tokens.reshape(TOK, -1), w_qkv)
    context = attention(
        row_pages.reshape(-1), last_fill.reshape(-1), page_order.reshape(-1),
        projected, kv_cache.reshape(PAGES, 2 * BLOCK, HD),
    )
    return output(context, w_out).reshape(ROWS, STEPS, -1)


def solution(mesh):
    placed = (
        P("grp", None, "tp"),
        P(("grp", "tp"), None),
        P(("grp", "tp"), None),
        P("grp", None, None, "tp"),
        P("grp", None),
        P("grp", None),
        P("grp", None),
    )
    return jax.shard_map(
        per_device, mesh=mesh, in_specs=placed, out_specs=P("grp", None, "tp"), check_vma=False
    )
```

time: 437 us -> 326 us (0.75)
  Pallas kernels: 0 us -> 322 us
  waiting for transfers between devices: 159 us -> 0 us
  local copies, waits for them, and re-layouts: 118 us -> 3.48 us
  matrix products: 64.8 us -> 0 us
  blocking collectives: 58.2 us -> 0 us
  other arithmetic: 19 us -> 0 us
  between operations: 13.3 us -> 0.09 us
    pallas_call x0 -> x3, Pallas kernels: none -> 322 us  [the longest x1 137 us: output(): pl.pallas_call(output_kernel, out_shape=jax.ShapeDtypeStruct((TOK, OC), b...]
    all_gather x3 -> x0, waiting for transfers between devices: 109 us -> none  [the longest x1 109 us: per_device(): lax.all_gather(qkv_part, 'grp', axis=0, tiled=True)]
    gather x5 -> x0, local copies, waits for them, and re-layouts: 92.6 us -> none  [the longest x4 86 us: attend_block(): gathered = cache_view[table_blk]]
    dot_general x10 -> x0, matrix products: 64.8 us -> none  [the longest x2 19.9 us: attend_block(): jnp.einsum('rkgst,rtkd->rskgd', cache_weight, flat_cache[:, :, 1], prefer...]
    all_to_all x2 -> x0, blocking collectives: 58.2 us -> none  [the longest x1 29.2 us: per_device(): lax.all_to_all(w_qkv, 'tp', split_axis=1, concat_axis=0, tiled=True)]
    reduce_scatter x1 -> x0, waiting for transfers between devices: 49.7 us -> none  [per_device(): lax.psum_scatter(terms.astype(jnp.bfloat16), 'tp', scatter_dimension=1, t...]
    reduce_sum x5 -> x0, other arithmetic: 10.4 us -> none  [the longest x4 5.97 us: attend_block(): row_total = jnp.sum(cache_prob, axis=-1) + jnp.sum(new_prob, axis=-1)]
    convert_element_type x1 -> x0, other arithmetic: 7.89 us -> none  [per_device(): normed = (widened * lax.rsqrt(jnp.mean(widened * widened, axis=2, keepdim...]
  transfers between devices with their start and end apart: 4 -> 0, of which waited for: 2 -> 0; matrix products, arithmetic and copies ran while one was open for 43% -> 0% of each run, Pallas kernels for 0% -> 0%
where the time goes in v1:
time: 326 us; the launch traced here: 325 us
  Pallas kernels  322 us (99%)
  local copies, waits for them, and re-layouts  3.48 us (1%)
    pallas_call x1, Pallas kernels, output(): pl.pallas_call(output_kernel, out_shape=jax.ShapeDtypeStruct((TOK, OC), b...  137 us
    pallas_call x1, Pallas kernels, project(): pl.pallas_call(project_kernel, out_shape=jax.ShapeDtypeStruct((TOK, QC),...  132 us
    pallas_call x1, Pallas kernels, attention(): pl.pallas_call(attention_kernel, out_shape=jax.ShapeDtypeStruct((TOK, OC)...  52.5 us

profile of v1, /device:TPU:12, one launch (start us, length us, event | category | flops | bytes accessed | tf_op | source)
XLA Modules:
  0.0 325.3 jit_solution(17433894248766398488)
XLA Ops:
  0.0 1.2 reshape.21.tok
  1.2 0.0 copy-start.4
  1.2 1.3 copy-done.4
  2.5 0.0 copy-start
  2.5 0.0 copy-start.1
  2.5 0.0 copy-start.2
  2.5 0.0 copy-start.3
  2.5 132.5 %project.1.proj = bf16[256,1280]{1,0:T(8,128)(2,1)S(1)} custom-call(bf16[256,1024]{1,0:T(8,128)(2,1)S(1)} %reshape.21.tok, bf16[64,10240]{1,0:T(8,128)(2,1)S(1)} %copy-done.4), custom_call_target="tpu_custom_call" | custom-call | flops 5368709120 | bytes 163840 | tf_op jit(solution)/shard_map/project/pallas_call | solution.py:486
  135.0 0.0 copy-done
  135.0 0.0 copy-done.1
  135.0 0.0 copy-done.2
  135.0 0.0 copy-done.3
  135.0 0.0 copy-start.5
  135.0 52.5 %attention.1.ctx = bf16[256,1024]{1,0:T(8,128)(2,1)S(1)} custom-call(s32[64]{0:T(128)S(1)} %bitcast.5, s32[64]{0:T(128)S(1)} %bitcast.6, s32[128]{0:T(128)S(1)} %bitcast.7, bf16[256,1280]{1,0:T(8,128)(2,1)S(1)} %project.1.proj, bf16[128,256,128]{2,1,0:T(8,128)(2,1)S(1)} %bitcast.4), custom_call_target="tpu_custom_call" | custom-call | tf_op jit(solution)/shard_map/attention/pallas_call | solution.py:191
  187.6 0.0 copy-done.5
  187.6 136.7 %output.1 = bf16[256,1024]{1,0:T(8,128)(2,1)S(1)} custom-call(bf16[256,1024]{1,0:T(8,128)(2,1)S(1)} %attention.1.ctx, bf16[64,8192]{1,0:T(8,128)(2,1)S(1)} %copy-done.5), custom_call_target="tpu_custom_call" | custom-call | flops 4294967296 | bytes 131072 | tf_op jit(solution)/shard_map/output/pallas_call | solution.py:598
  324.3 1.0 reshape.23
Async XLA Ops:
  1.2 1.3 copy-start.4
  2.5 132.5 %copy-start = (bf16[128,128,2,128]{3,2,1,0:T(2,128)(2,1)S(1)}, bf16[128,128,2,128]{3,2,1,0:T(2,128)(2,1)}, u32[]{:S(2)}) copy-start(bf16[128,128,2,128]{3,2,1,0:T(2,128)(2,1)} %param.10) | copy-start | bytes 25165828
  2.5 132.5 %copy-start.1 = (s32[1,64]{1,0:T(1,128)S(1)}, s32[1,64]{1,0:T(1,128)}, u32[]{:S(2)}) copy-start(s32[1,64]{1,0:T(1,128)} %param.11) | copy-start | bytes 772
  2.5 132.5 %copy-start.2 = (s32[1,64]{1,0:T(1,128)S(1)}, s32[1,64]{1,0:T(1,128)}, u32[]{:S(2)}) copy-start(s32[1,64]{1,0:T(1,128)} %param.12) | copy-start | bytes 772
  2.5 132.5 %copy-start.3 = (s32[1,128]{1,0:T(1,128)S(1)}, s32[1,128]{1,0:T(1,128)}, u32[]{:S(2)}) copy-start(s32[1,128]{1,0:T(1,128)} %param.13) | copy-start | bytes 1540
  135.0 52.6 %copy-start.5 = (bf16[64,8192]{1,0:T(8,128)(2,1)S(1)}, bf16[64,8192]{1,0:T(8,128)(2,1)}, u32[]{:S(2)}) copy-start(bf16[64,8192]{1,0:T(8,128)(2,1)} %w.3) | copy-start | bytes 3145732

commit v2 on v0

v2 whole, which is shorter than its diff:
```python
import jax
import jax.numpy as jnp
from jax import lax
from jax.experimental import pallas as pl
from jax.experimental.pallas import tpu as pltpu
from jax.sharding import PartitionSpec as P

HD = 128
STEPS = 4
PER_GROUP = 8
BLOCK = 128
ROWS = 64
PAGES = 128
TOK = ROWS * STEPS
D = 8192
TP = 8
QC = 1280
OC = 1024
EPS = 1e-05
SCALE = HD ** (-0.5)
MESH = pl.DeviceIdType.MESH
MIB = 1 << 20


def page_maps(row_pages, last_fill, order, of_page, of_row, valid):
    f32 = jnp.float32
    none = jnp.zeros((1, PAGES - ROWS), f32)
    pages = jnp.concatenate([row_pages[...].astype(f32), none], axis=1)
    fill = jnp.concatenate([last_fill[...].astype(f32), none], axis=1)
    down = lax.broadcasted_iota(jnp.int32, (PAGES, PAGES), 0)
    along = lax.broadcasted_iota(jnp.int32, (PAGES, PAGES), 1)
    upto = jnp.where(down <= along, 1.0, 0.0)
    end = jnp.dot(jnp.broadcast_to(pages, (8, PAGES)), upto, preferred_element_type=f32)[0:1]
    place = jnp.sum(
        jnp.where(order[...] == down, along.astype(f32), 0.0), axis=1, keepdims=True
    )
    mine = (place >= end - pages) & (place < end)
    used = jnp.where(place == end - 1.0, fill, float(BLOCK))
    valid[...] = jnp.broadcast_to(
        jnp.sum(jnp.where(mine, used, 0.0), axis=1, keepdims=True), (PAGES, PAGES)
    )
    found = jnp.where(mine, 1.0, 0.0)
    of_page[...] = found
    of_row[...] = found.T[:ROWS]


def page_queries(pf, of_page, q_pg):
    def head(a, _):
        for step in range(STEPS):
            q = pf[a, pl.ds(step, ROWS, stride=STEPS), :]
            q_pg[pl.ds(a * STEPS + step, PAGES, stride=32), :] = jnp.dot(
                of_page[:, :ROWS], q, preferred_element_type=jnp.float32
            )
        return 0

    lax.fori_loop(0, PER_GROUP, head, 0)


def cached_tokens(cache, q_pg, valid, m_all, l_all, o_pg):
    n_at = 16
    lane = lax.broadcasted_iota(jnp.int32, (1, 2 * BLOCK), 1)
    lane = jnp.where((lane & 1) == 0, lane.astype(jnp.float32), 1e6)
    page = lax.broadcasted_iota(jnp.int32, (32, PAGES), 1)

    def some(n, run):
        m_run, l_run = run
        slots = [n * n_at + k for k in range(n_at)]
        pages = [cache[i] for i in slots]
        rows = [pl.ds(pl.multiple_of(i * 32, 32), 32) for i in slots]
        raw = [
            lax.dot_general(
                q_pg[at, :].astype(jnp.bfloat16), kv, (((1,), (1,)), ((), ())),
                preferred_element_type=jnp.float32,
            )
            for at, kv in zip(rows, pages)
        ]
        ends = [valid[pl.ds(i, 1), :] * 2.0 for i in slots]
        ends = [jnp.concatenate([e, e], axis=1) for e in ends]
        raw = [s * SCALE + jnp.where(lane < e, 0.0, -jnp.inf) for s, e in zip(raw, ends)]
        tops = [jnp.max(s, axis=1, keepdims=True) for s in raw]
        probs = [jnp.exp(s - m) for s, m in zip(raw, tops)]
        totals = [jnp.sum(p, axis=1, keepdims=True) for p in probs]
        moved = [pltpu.roll(p, 1, 1).astype(jnp.bfloat16) for p in probs]
        outs = [
            jnp.dot(w, kv, preferred_element_type=jnp.float32)
            for w, kv in zip(moved, pages)
        ]
        for k, i in enumerate(slots):
            o_pg[rows[k], :] = outs[k]
            m_run = jnp.where(page == i, tops[k], m_run)
            l_run = jnp.where(page == i, totals[k], l_run)
        return m_run, l_run

    zero = jnp.zeros((32, PAGES), jnp.float32)
    m_all[...], l_all[...] = lax.fori_loop(0, PAGES // n_at, some, (zero, zero))


def join_pages(pf, of_row, m_all, l_all, o_pg, joined):
    def head(a, _):
        for step in range(STEPS):
            h = a * STEPS + step
            rows = pl.ds(step, ROWS, stride=STEPS)
            q = pf[a, rows, :]
            fresh = [
                jnp.sum(
                    q * pf[PER_GROUP, pl.ds(u, ROWS, stride=STEPS), :], axis=1, keepdims=True
                )
                * SCALE
                for u in range(step + 1)
            ]
            tops = jnp.where(of_row[...] > 0.5, m_all[pl.ds(h, 1), :], -jnp.inf)
            top = jnp.max(tops, axis=1, keepdims=True)
            for s in fresh:
                top = jnp.maximum(top, s)
            share = jnp.exp(tops - top)
            total = jnp.sum(share * l_all[pl.ds(h, 1), :], axis=1, keepdims=True)
            out = jnp.dot(
                share, o_pg[pl.ds(h, PAGES, stride=32), :],
                preferred_element_type=jnp.float32, precision=lax.Precision.HIGHEST,
            )
            for u, s in enumerate(fresh):
                p = jnp.exp(s - top)
                total = total + p
                out = out + p * pf[PER_GROUP + 1, pl.ds(u, ROWS, stride=STEPS), :]
            joined[a, rows, :] = out / total
        return 0

    lax.fori_loop(0, PER_GROUP, head, 0)


class Place:
    def __init__(self):
        g, t = lax.axis_index("grp"), lax.axis_index("tp")
        self.g, self.t = g, t
        self.core = g % 2
        self.z = (g // 2) % 4
        self.yh = g // 8
        self.yl = t // 4
        self.x = t % 4
        self.y = self.yh * 2 + self.yl
        self.zm = (self.z + 3) % 4
        self.zp = (self.z + 1) % 4
        self.z2 = (self.z + 2) % 4

    def at(self, y=None, z=None, x=None, core=None):
        y = self.y if y is None else y
        z = self.z if z is None else z
        x = self.x if x is None else x
        core = self.core if core is None else core
        return ((y // 2) * 4 + z) * 2 + core, (y % 2) * 4 + x


def greet(me):
    barrier = pltpu.get_barrier_semaphore()

    def signal(who):
        pl.semaphore_signal(barrier, inc=1, device_id=who, device_id_type=MESH)

    def plane(k, _):
        signal(me.at(y=(me.y + k // 4) % 4, x=(me.x + k) % 4))
        return 0

    lax.fori_loop(1, 16, plane, 0)
    signal(me.at(z=me.zp))
    signal(me.at(z=me.zm))
    for k in range(4):
        signal(me.at(y=(me.y + k) % 4, core=1 - me.core))
    for k in range(1, 4):
        signal(me.at(x=(me.x + k) % 4, core=1 - me.core))
    pl.semaphore_wait(barrier, 24)


def remote(src, dst, sent, got, who):
    return pltpu.make_async_remote_copy(
        src, dst, sent, got, device_id=who, device_id_type=MESH
    )


class Ring:
    def __init__(self, me, count, order, slot, up, down, got):
        self.me, self.count, self.order, self.slot = me, count, order, slot
        self.up, self.down, self.got = up, down, got

    def send_up(self, z, p, k):
        return remote(
            self.slot(z, p), self.slot(z, p), self.up.at[k], self.got.at[z, p],
            self.me.at(z=self.me.zp),
        )

    def send_down(self, z, p, k):
        return remote(
            self.slot(z, p), self.slot(z, p), self.down.at[k], self.got.at[z, p],
            self.me.at(z=self.me.zm),
        )

    def arrived(self, z, p):
        self.send_up(z, p, 0).wait_recv()

    def pass_own(self, local):
        def send(k):
            p = self.order(k)
            self.send_up(self.me.z, p, k).start()
            self.send_down(self.me.z, p, k).start()

        for k, copy in enumerate(local):
            copy.wait()
            send(k)

        def one(k, _):
            self.arrived(self.me.z, self.order(k))
            send(k)
            return 0

        lax.fori_loop(len(local), self.count, one, 0)

    def pass_on(self, low, high):
        me = self.me

        def two(n, _):
            p, q = self.order(2 * n), self.order(2 * n + 1)
            self.arrived(me.zm, p)
            self.send_up(me.zm, p, self.count + n).start()
            self.arrived(me.zp, p)
            self.arrived(me.zp, q)
            self.send_down(me.zp, q, self.count + n).start()
            self.arrived(me.zm, q)
            return 0

        lax.fori_loop(low, high, two, 0)

    def last(self):
        def one(k, _):
            self.arrived(self.me.z2, self.order(k))
            return 0

        lax.fori_loop(0, self.count, one, 0)

    def finish(self):
        def one(k, _):
            p = k % self.count
            self.send_up(self.me.z, p, k).wait_send()
            self.send_down(self.me.z, p, k).wait_send()
            return 0

        lax.fori_loop(0, self.count + self.count // 2, one, 0)


def ring_sems(count):
    dma = pltpu.SemaphoreType.DMA
    more = count + count // 2
    return [dma((count,)), dma((more,)), dma((more,)), dma((4, count))]


def layer_kernel(
    row_pages, last_fill, order, tok, w_qkv, w_out, cache_hbm, out,
    xbuf, qbuf, obuf, acc, squares, half_sent, half_got, full_sent, full_got,
    sq_half, sq_sum, sq_full,
    cache, pf, of_page, of_row, valid, q_pg, m_all, l_all, o_pg, joined,
    mine, ctx, o_acc, keep, give, taken, sums, final,
    own_sem, cache_sem,
    q_sent, q_up, q_down, q_got,
    w_sent, w_up, w_down, w_got,
    x_sent, x_up, x_down, x_got,
    sq_s, sq_g, h_s, h_g, f_s, f_g,
    c_up, c_down, c_core, c_got,
    y_s, y_g, e_s, e_g,
):
    me = Place()
    c = me.core
    other = me.at(core=1 - c)
    right, left = me.at(x=(me.x + 1) % 4), me.at(x=(me.x + 3) % 4)
    xl, xr, x2 = (me.x + 3) % 4, (me.x + 1) % 4, (me.x + 2) % 4
    far = me.at(y=(me.y + 2) % 4)
    near = me.at(y=me.yh * 2 + 1 - me.yl)
    greet(me)

    piece = me.yh * 2 + c

    def half(h):
        return tok.at[:, pl.ds(pl.multiple_of(h * 512, 512), 512)]

    def x_first(n):
        h = (c + n % 2) % 2
        who = me.at(y=me.yl * 2 + (me.yl + n // 2) % 2, core=h)
        return remote(half(h), xbuf.at[me.x, piece], x_sent.at[n], x_got.at[me.x, piece], who)

    stays = me.yh == me.yl

    x_here = pltpu.make_async_copy(half(c), xbuf.at[me.x, piece], own_sem.at[0])

    @pl.when(stays)
    def _():
        x_here.start()

    @pl.when(jnp.logical_not(stays))
    def _():
        x_first(0).start()

    for n in range(1, 4):
        x_first(n).start()

    def q_columns(t):
        return w_qkv.at[:, pl.ds(pl.multiple_of(t * QC, QC), QC)]

    def q_plane(k):
        t = (me.t + k) % TP
        return remote(q_columns(t), qbuf.at[me.z, me.t], q_sent.at[k], q_got.at[me.z, me.t], (me.g, t))

    def q_start(k, _):
        q_plane(k).start()
        return 0

    q_here = [pltpu.make_async_copy(q_columns(me.t), qbuf.at[me.z, me.t], own_sem.at[1])]
    q_here[0].start()
    lax.fori_loop(1, TP, q_start, 0)
    q_ring = Ring(
        me, TP, lambda k: (me.t + TP - k) % TP, lambda z, p: qbuf.at[z, p], q_up, q_down, q_got
    )

    def cached(n):
        rows = pl.ds(n * 16, 16)
        return pltpu.make_async_copy(cache_hbm.at[rows], cache.at[rows], cache_sem.at[n])

    for n in range(8):
        cached(n).start()

    def x_along(x, p, who, sem):
        return remote(xbuf.at[x, p], xbuf.at[x, p], sem, x_got.at[x, p], who)

    for n in range(4):
        p = (piece + n) % 4
        if n:
            x_along(me.x, p, right, x_up.at[0]).wait_recv()
        else:

            @pl.when(stays)
            def _():
                x_here.wait()

            @pl.when(jnp.logical_not(stays))
            def _():
                x_along(me.x, piece, right, x_up.at[0]).wait_recv()

        x_along(me.x, p, right, x_up.at[n]).start()
        x_along(me.x, p, left, x_down.at[n]).start()

    def w_columns(yl, n):
        return w_out.at[:, pl.ds(pl.multiple_of((yl * 4 + n) * OC, OC), OC)]

    def w_slot(z, p):
        return obuf.at[z, p // 4, p % 4]

    def w_plane(k):
        y, n = (me.y + k // 4) % 4, k % 4
        p = me.y * 4 + n
        return remote(w_columns(y % 2, n), w_slot(me.z, p), w_sent.at[k], w_got.at[me.z, p], me.at(y=y))

    def w_start(k, _):
        w_plane(k).start()
        return 0

    w_here = [
        pltpu.make_async_copy(w_columns(me.yl, n), w_slot(me.z, me.y * 4 + n), own_sem.at[2 + n])
        for n in range(4)
    ]
    for copy in w_here:
        copy.start()
    lax.fori_loop(4, 16, w_start, 0)
    w_ring = Ring(
        me, 16, lambda k: ((me.y + 4 - k // 4) % 4) * 4 + k % 4, w_slot, w_up, w_down, w_got
    )

    q_ring.pass_own(q_here)
    for n in range(4):
        x_along(xl, n, right, x_up.at[0]).wait_recv()
        x_along(xr, n, right, x_up.at[0]).wait_recv()
        if n < 2:
            x_along(xl, n, right, x_up.at[4 + n]).start()
        else:
            x_along(xr, n, left, x_down.at[2 + n]).start()
    q_ring.pass_on(0, 4)
    page_maps(row_pages, last_fill, order, of_page, of_row, valid)
    w_ring.pass_own(w_here)
    for n in range(4):
        x_along(x2, n, right, x_up.at[0]).wait_recv()

    squares[...] = jnp.zeros_like(squares)

    def square(n, _):
        x, p, r = n // 16, (n // 4) % 4, n % 4
        v = xbuf[x, p, pl.ds(pl.multiple_of(r * 64, 64), 64), :].astype(jnp.float32)
        v = v * v
        v = v[:, :128] + v[:, 128:256] + v[:, 256:384] + v[:, 384:]
        squares[p, pl.ds(pl.multiple_of(r * 64, 64), 64), :] += v
        return 0

    lax.fori_loop(0, 64, square, 0)
    sq_swap = [
        remote(squares.at[2 * n + 1 - c], sq_half.at[n], sq_s.at[n], sq_g.at[n], other)
        for n in range(2)
    ]
    for copy in sq_swap:
        copy.start()

    def product(z, n):
        cols = pl.ds(pl.multiple_of(n * 256, 256), 256)
        xs = xbuf[z].reshape(4 * TOK, 512)
        ws = qbuf[z, :, :, cols].reshape(512, 256)
        return cols, jnp.dot(xs, ws, preferred_element_type=jnp.float32)

    def multiply(z, fresh=False):
        def tile(n, _):
            cols, value = product(z, n)
            acc[:, cols] = value if fresh else acc[:, cols] + value
            return 0

        lax.fori_loop(0, QC // 256, tile, 0)

    multiply(me.z, True)
    for copy in sq_swap:
        copy.wait_recv()
    for n in range(2):
        sq_sum[n] = squares[2 * n + c] + sq_half[n]
    sq_far = remote(sq_sum.at[1 - me.yh], sq_full, sq_s.at[2], sq_g.at[2], far)
    sq_far.start()
    multiply(me.zm)
    multiply(me.zp)
    q_ring.last()

    def half_copy(n):
        return remote(half_sent.at[n], half_got.at[n], h_s.at[n], h_g.at[n], other)

    def full_copy(n):
        return remote(full_sent.at[n], full_got.at[n], f_s.at[n], f_g.at[n], far)

    def block(p):
        return pl.ds(pl.multiple_of(p * TOK, TOK), TOK)

    def last_tile(n):
        cols, value = product(me.z2, n)
        acc[:, cols] += value
        for m in range(2):
            half_sent[n, m] = acc[block(2 * m + 1 - c), cols].astype(jnp.bfloat16)
        half_copy(n).start()

    for n in range(QC // 256):
        last_tile(n)

    def join_half(n):
        cols = pl.ds(pl.multiple_of(n * 256, 256), 256)
        half_copy(n).wait_recv()
        theirs = acc[block(2 * (1 - me.yh) + c), cols] + half_got[n, 1 - me.yh].astype(jnp.float32)
        full_sent[n] = theirs.astype(jnp.bfloat16)
        full_copy(n).start()
        acc[block(piece), cols] += half_got[n, me.yh].astype(jnp.float32)

    for n in range(QC // 256):
        join_half(n)
    sq_far.wait_recv()
    mean = jnp.sum(sq_sum[me.yh] + sq_full[...], axis=1, keepdims=True) * (1.0 / D)
    gain = lax.rsqrt(mean + EPS)

    def join_full(n):
        cols = pl.ds(pl.multiple_of(n * 256, 256), 256)
        full_copy(n).wait_recv()
        total = acc[block(piece), cols] + full_got[n].astype(jnp.float32)
        total = (total * gain).astype(jnp.bfloat16).astype(jnp.float32)
        pf[2 * n], pf[2 * n + 1] = total[:, :HD], total[:, HD:]

    for n in range(QC // 256):
        join_full(n)

    page_queries(pf, of_page, q_pg)
    for n in range(8):
        cached(n).wait()
    cached_tokens(cache, q_pg, valid, m_all, l_all, o_pg)
    join_pages(pf, of_row, m_all, l_all, o_pg, joined)
    for a in range(PER_GROUP):
        mine[:, pl.ds(a * HD, HD)] = joined[a].astype(jnp.bfloat16)

    def c_along(x, core, h, sem, who):
        slot = ctx.at[x, core, h]
        return remote(slot, slot, sem, c_got.at[x, core, h], who)

    def c_first(h, sem, who):
        slot = ctx.at[me.x, c, h]
        return remote(mine.at[pl.ds(h * 128, 128)], slot, sem, c_got.at[me.x, c, h], who)

    c_here = [
        pltpu.make_async_copy(
            mine.at[pl.ds(h * 128, 128)], ctx.at[me.x, c, h], own_sem.at[6 + h]
        )
        for h in range(2)
    ]
    for h in range(2):
        c_first(h, c_up.at[h], right).start()
        c_first(h, c_down.at[h], left).start()
        c_first(h, c_core.at[h], other).start()
        c_here[h].start()
    w_ring.pass_on(0, 8)
    for h in range(2):
        c_along(xl, c, h, c_up.at[0], right).wait_recv()
        if h == 0:
            c_along(xl, c, h, c_up.at[2], right).start()
        c_along(xl, c, h, c_core.at[2 + h], other).start()
        c_along(xr, c, h, c_up.at[0], right).wait_recv()
        if h == 1:
            c_along(xr, c, h, c_down.at[2], left).start()
        c_along(xr, c, h, c_core.at[4 + h], other).start()
    for h in range(2):
        c_along(x2, c, h, c_up.at[0], right).wait_recv()
        c_along(x2, c, h, c_core.at[6 + h], other).start()
    for x in (me.x, xl, xr, x2):
        for h in range(2):
            c_along(x, 1 - c, h, c_up.at[0], right).wait_recv()
    for copy in c_here:
        copy.wait()

    def y_copy(j):
        return remote(give.at[j], taken.at[j], y_s.at[j], y_g.at[j], near)

    def features(j, z):
        def term(n, _):
            ws = obuf[z, :, n].reshape(256, OC)
            xs = ctx[n].reshape(2 * TOK, OC)
            value = lax.dot_general(
                xs, ws, (((1,), (1,)), ((), ())), preferred_element_type=jnp.float32
            )
            o_acc[...] = jnp.where(n == 0, value, o_acc[...] + value)
            return 0

        lax.fori_loop(0, 4, term, 0)
        keep[j] = o_acc[:, pl.ds(pl.multiple_of(me.yl * 128, 128), 128)]
        give[j] = o_acc[:, pl.ds(pl.multiple_of((1 - me.yl) * 128, 128), 128)].astype(jnp.bfloat16)
        y_copy(j).start()

    def e_copy(j, z, m):
        core = (c + m) % 2
        return remote(
            sums.at[j, core], final.at[c, me.x], e_s.at[j, m], e_g.at[c, me.x], me.at(x=z, core=core)
        )

    def spread(j, z):
        y_copy(j).wait_recv()
        total = keep[j] + taken[j].astype(jnp.float32)
        sums[j] = total.astype(jnp.bfloat16).reshape(2, TOK, 128)
        e_copy(j, z, 1).start()

        @pl.when(z != me.x)
        def _():
            e_copy(j, z, 0).start()

        @pl.when(z == me.x)
        def _():
            here = pltpu.make_async_copy(sums.at[j, c], final.at[c, me.x], own_sem.at[8])
            here.start()
            here.wait()

    features(0, me.z)
    features(1, me.zm)
    spread(0, me.z)
    features(2, me.zp)
    spread(1, me.zm)
    w_ring.last()
    features(3, me.z2)
    spread(2, me.zp)
    spread(3, me.z2)

    @pl.when(jnp.logical_not(stays))
    def _():
        x_first(0).wait_send()

    for n in range(1, 4):
        x_first(n).wait_send()
    for n in range(6):
        x_along(me.x, 0, right, x_up.at[n]).wait_send()
        x_along(me.x, 0, left, x_down.at[n]).wait_send()

    def q_done(k, _):
        q_plane(k).wait_send()
        return 0

    def w_done(k, _):
        w_plane(k).wait_send()
        return 0

    lax.fori_loop(1, TP, q_done, 0)
    lax.fori_loop(4, 16, w_done, 0)
    q_ring.finish()
    w_ring.finish()
    for copy in sq_swap:
        copy.wait_send()
    sq_far.wait_send()
    for n in range(QC // 256):
        half_copy(n).wait_send()
        full_copy(n).wait_send()
    for n in range(3):
        c_along(me.x, c, 0, c_up.at[n], right).wait_send()
        c_along(me.x, c, 0, c_down.at[n], left).wait_send()
    for n in range(8):
        c_along(me.x, c, 0, c_core.at[n], other).wait_send()
    for j, z in enumerate((me.z, me.zm, me.zp, me.z2)):
        y_copy(j).wait_send()
        e_copy(j, z, 1).wait_send()

        @pl.when(z != me.x)
        def _(j=j, z=z):
            e_copy(j, z, 0).wait_send()

    for k in range(8):
        core, x = (c + k // 4) % 2, (me.x + k) % 4
        if k:
            remote(final.at[core, x], final.at[core, x], e_s.at[0, 0], e_g.at[core, x], other).wait_recv()

    for core in range(2):
        for yl in range(2):
            out[:, pl.ds(core * 512 + yl * 256, 256)] = jnp.concatenate(
                [final[core, x, :, pl.ds(yl * 64, 64)] for x in range(4)], axis=1
            )


def layer(row_pages, last_fill, order, tokens, w_qkv, w_out, cache):
    dma = pltpu.SemaphoreType.DMA
    inside = pl.BlockSpec(memory_space=pltpu.VMEM)
    anywhere = pl.BlockSpec(memory_space=pl.ANY)
    f32, bf16 = jnp.float32, jnp.bfloat16
    tiles = QC // 256

    def vmem(dtype, *shape):
        return pltpu.VMEM(shape, dtype)

    return pl.pallas_call(
        layer_kernel,
        out_shape=jax.ShapeDtypeStruct((TOK, OC), bf16),
        in_specs=[inside] * 3 + [anywhere] * 4,
        out_specs=pl.BlockSpec(memory_space=pltpu.VMEM),
        scratch_shapes=[
            vmem(bf16, 4, 4, TOK, 512),
            vmem(bf16, 4, TP, 64, QC),
            vmem(bf16, 4, 4, 4, 64, OC),
            vmem(f32, 4 * TOK, QC),
            vmem(f32, 4, TOK, 128),
            vmem(bf16, tiles, 2, TOK, 256),
            vmem(bf16, tiles, 2, TOK, 256),
            vmem(bf16, tiles, TOK, 256),
            vmem(bf16, tiles, TOK, 256),
            vmem(f32, 2, TOK, 128),
            vmem(f32, 2, TOK, 128),
            vmem(f32, TOK, 128),
            vmem(bf16, PAGES, 2 * BLOCK, HD),
            vmem(f32, PER_GROUP + 2, TOK, HD),
            vmem(f32, PAGES, PAGES),
            vmem(f32, ROWS, PAGES),
            vmem(f32, PAGES, PAGES),
            vmem(f32, PAGES * 32, HD),
            vmem(f32, 32, PAGES),
            vmem(f32, 32, PAGES),
            vmem(f32, PAGES * 32, HD),
            vmem(f32, PER_GROUP, TOK, HD),
            vmem(bf16, TOK, OC),
            vmem(bf16, 4, 2, 2, 128, OC),
            vmem(f32, 2 * TOK, 256),
            vmem(f32, 4, 2 * TOK, 128),
            vmem(bf16, 4, 2 * TOK, 128),
            vmem(bf16, 4, 2 * TOK, 128),
            vmem(bf16, 4, 2, TOK, 128),
            vmem(bf16, 2, 4, TOK, 128),
            dma((9,)),
            dma((8,)),
        ]
        + ring_sems(TP)
        + ring_sems(16)
        + [dma((4,)), dma((6,)), dma((6,)), dma((4, 4))]
        + [dma((3,)), dma((3,)), dma((tiles,)), dma((tiles,)), dma((tiles,)), dma((tiles,))]
        + [dma((3,)), dma((3,)), dma((8,)), dma((4, 2, 2))]
        + [dma((4,)), dma((4,)), dma((4, 2)), dma((2, 4))],
        compiler_params=pltpu.CompilerParams(
            collective_id=0, has_side_effects=True, vmem_limit_bytes=60 * MIB
        ),
        cost_estimate=pl.CostEstimate(
            flops=2 * TOK * D * (QC + OC), bytes_accessed=16 * MIB, transcendentals=0
        ),
        name="layer",
    )(row_pages, last_fill, order, tokens, w_qkv, w_out, cache)


def per_device(tokens, w_qkv, w_out, kv_cache, row_pages, last_fill, page_order):
    mixed = layer(
        row_pages, last_fill, page_order,
        tokens.reshape(TOK, -1), w_qkv, w_out, kv_cache.reshape(PAGES, 2 * BLOCK, HD),
    )
    return mixed.reshape(ROWS, STEPS, -1)


def solution(mesh):
    placed = (
        P("grp", None, "tp"),
        P(("grp", "tp"), None),
        P(("grp", "tp"), None),
        P("grp", None, None, "tp"),
        P("grp", None),
        P("grp", None),
        P("grp", None),
    )
    return jax.shard_map(
        per_device, mesh=mesh, in_specs=placed, out_specs=P("grp", None, "tp"), check_vma=False
    )
```

time: 437 us -> 164 us (0.38)
  Pallas kernels: 0 us -> 160 us
  waiting for transfers between devices: 159 us -> 0 us
  local copies, waits for them, and re-layouts: 118 us -> 3.99 us
  matrix products: 64.8 us -> 0 us
  blocking collectives: 58.2 us -> 0 us
  other arithmetic: 19 us -> 0 us
  between operations: 13.3 us -> 0.01 us
    pallas_call x0 -> x1, Pallas kernels: none -> 160 us  [layer(): pl.pallas_call(layer_kernel, out_shape=jax.ShapeDtypeStruct((TOK, OC), bf...]
    all_gather x3 -> x0, waiting for transfers between devices: 109 us -> none  [the longest x1 109 us: per_device(): lax.all_gather(qkv_part, 'grp', axis=0, tiled=True)]
    gather x5 -> x0, local copies, waits for them, and re-layouts: 92.6 us -> none  [the longest x4 86 us: attend_block(): gathered = cache_view[table_blk]]
    dot_general x10 -> x0, matrix products: 64.8 us -> none  [the longest x2 19.9 us: attend_block(): jnp.einsum('rkgst,rtkd->rskgd', cache_weight, flat_cache[:, :, 1], prefer...]
    all_to_all x2 -> x0, blocking collectives: 58.2 us -> none  [the longest x1 29.2 us: per_device(): lax.all_to_all(w_qkv, 'tp', split_axis=1, concat_axis=0, tiled=True)]
    reduce_scatter x1 -> x0, waiting for transfers between devices: 49.7 us -> none  [per_device(): lax.psum_scatter(terms.astype(jnp.bfloat16), 'tp', scatter_dimension=1, t...]
    reduce_sum x5 -> x0, other arithmetic: 10.4 us -> none  [the longest x4 5.97 us: attend_block(): row_total = jnp.sum(cache_prob, axis=-1) + jnp.sum(new_prob, axis=-1)]
    unnamed x9 -> x0, local copies, waits for them, and re-layouts: 9.17 us -> none
  transfers between devices with their start and end apart: 4 -> 0, of which waited for: 2 -> 0; matrix products, arithmetic and copies ran while one was open for 43% -> 0% of each run, Pallas kernels for 0% -> 0%
where the time goes in v2:
time: 164 us
  Pallas kernels  160 us (98%)
  local copies, waits for them, and re-layouts  3.99 us (2%)
    pallas_call x1, Pallas kernels, layer(): pl.pallas_call(layer_kernel, out_shape=jax.ShapeDtypeStruct((TOK, OC), bf...  160 us

profile of v2, /device:TPU:12, one launch (start us, length us, event | category | flops | bytes accessed | tf_op | source)
XLA Modules:
  0.0 163.8 jit_solution(18358267333821724644)
XLA Ops:
  0.0 2.0 %reshape.9.tok = bf16[256,1024]{1,0:T(8,128)(2,1)} reshape(bf16[64,4,1024]{2,1,0:T(4,128)(2,1)} %param.7) | data formatting | bytes 1048576 | tf_op jit(solution)/shard_map/reshape | solution.py:690
  2.0 159.8 %layer.1 = bf16[256,1024]{1,0:T(8,128)(2,1)} custom-call(s32[1,64]{1,0:T(1,128)} %row_pages.1, s32[1,64]{1,0:T(1,128)} %last_fill.1, s32[1,128]{1,0:T(1,128)} %order.1, bf16[256,1024]{1,0:T(8,128)(2,1)} %reshape.9.tok, bf16[64,10240]{1,0:T(8,128)(2,1)} %w_qkv.1, bf16[64,8192]{1,0:T(8,128)(2,1)} %w_out.1, bf16[128,256,128]{2,1,0:T(8,128)(2,1)} %bitcast.1), custom_call_target="tpu_custom_call" | custom-call | flops 9663676416 | bytes 16777216 | tf_op jit(solution)/shard_map/layer/pallas_call | solution.py:632
  161.8 2.0 %reshape.11 = bf16[64,4,1024]{2,1,0:T(4,128)(2,1)} reshape(bf16[256,1024]{1,0:T(8,128)(2,1)} %layer.1) | data formatting | bytes 1048576 | tf_op jit(solution)/shard_map/reshape | solution.py:692

commit v3 on v2

--- a/solution.py
+++ b/solution.py
@@ -196,22 +196,23 @@
     def arrived(self, z, p):
         self.send_up(z, p, 0).wait_recv()
 
-    def pass_own(self, local):
-        def send(k):
-            p = self.order(k)
-            self.send_up(self.me.z, p, k).start()
-            self.send_down(self.me.z, p, k).start()
-
+    def send(self, k):
+        p = self.order(k)
+        self.send_up(self.me.z, p, k).start()
+        self.send_down(self.me.z, p, k).start()
+
+    def pass_local(self, local):
         for k, copy in enumerate(local):
             copy.wait()
-            send(k)
-
+            self.send(k)
+
+    def pass_own(self, low):
         def one(k, _):
             self.arrived(self.me.z, self.order(k))
-            send(k)
+            self.send(k)
             return 0
 
-        lax.fori_loop(len(local), self.count, one, 0)
+        lax.fori_loop(low, self.count, one, 0)
 
     def pass_on(self, low, high):
         me = self.me
@@ -317,6 +318,8 @@
         me, TP, lambda k: (me.t + TP - k) % TP, lambda z, p: qbuf.at[z, p], q_up, q_down, q_got
     )
 
+    q_ring.pass_local(q_here)
+
     def cached(n):
         rows = pl.ds(n * 16, 16)
         return pltpu.make_async_copy(cache_hbm.at[rows], cache.at[rows], cache_sem.at[n])
@@ -370,7 +373,21 @@
         me, 16, lambda k: ((me.y + 4 - k // 4) % 4) * 4 + k % 4, w_slot, w_up, w_down, w_got
     )
 
-    q_ring.pass_own(q_here)
+
+    def square(x, fresh=False):
+        def part(n, _):
+            p, at = n // 4, pl.ds(pl.multiple_of((n % 4) * 64, 64), 64)
+            v = xbuf[x, p, at, :].astype(jnp.float32)
+            v = v * v
+            v = v[:, :128] + v[:, 128:256] + v[:, 256:384] + v[:, 384:]
+            squares[p, at, :] = v if fresh else squares[p, at, :] + v
+            return 0
+
+        lax.fori_loop(0, 16, part, 0)
+
+    square(me.x, True)
+    page_maps(row_pages, last_fill, order, of_page, of_row, valid)
+    q_ring.pass_own(1)
     for n in range(4):
         x_along(xl, n, right, x_up.at[0]).wait_recv()
         x_along(xr, n, right, x_up.at[0]).wait_recv()
@@ -379,52 +396,48 @@
         else:
             x_along(xr, n, left, x_down.at[2 + n]).start()
     q_ring.pass_on(0, 4)
-    page_maps(row_pages, last_fill, order, of_page, of_row, valid)
-    w_ring.pass_own(w_here)
+    w_ring.pass_local(w_here)
+    w_ring.pass_own(4)
+
+    def product(z, n):
+        cols = pl.ds(pl.multiple_of(n * 256, 256), 256)
+        xs = xbuf[z].reshape(4 * TOK, 512)
+        ws = qbuf[z, :, :, cols].reshape(512, 256)
+        return cols, jnp.dot(xs, ws, preferred_element_type=jnp.float32)
+
+    def multiply(z, fresh=False):
+        def tile(n, _):
+            cols, value = product(z, n)
+            acc[:, cols] = value if fresh else acc[:, cols] + value
+            return 0
+
+        lax.fori_loop(0, QC // 256, tile, 0)
+
+    gap = (me.z2 + 4 - x2) % 4
+    one = (x2 + jnp.where(gap == 1, 2, 1)) % 4
+    two = (x2 + jnp.where((gap == 0) | (gap == 3), 2, 3)) % 4
+    three = jnp.where(gap == 0, (x2 + 3) % 4, x2)
+    four = me.z2
+    multiply(one, True)
+    square(xl)
+    square(xr)
+    multiply(two)
     for n in range(4):
         x_along(x2, n, right, x_up.at[0]).wait_recv()
-
-    squares[...] = jnp.zeros_like(squares)
-
-    def square(n, _):
-        x, p, r = n // 16, (n // 4) % 4, n % 4
-        v = xbuf[x, p, pl.ds(pl.multiple_of(r * 64, 64), 64), :].astype(jnp.float32)
-        v = v * v
-        v = v[:, :128] + v[:, 128:256] + v[:, 256:384] + v[:, 384:]
-        squares[p, pl.ds(pl.multiple_of(r * 64, 64), 64), :] += v
-        return 0
-
-    lax.fori_loop(0, 64, square, 0)
+    square(x2)
     sq_swap = [
         remote(squares.at[2 * n + 1 - c], sq_half.at[n], sq_s.at[n], sq_g.at[n], other)
         for n in range(2)
     ]
     for copy in sq_swap:
         copy.start()
-
-    def product(z, n):
-        cols = pl.ds(pl.multiple_of(n * 256, 256), 256)
-        xs = xbuf[z].reshape(4 * TOK, 512)
-        ws = qbuf[z, :, :, cols].reshape(512, 256)
-        return cols, jnp.dot(xs, ws, preferred_element_type=jnp.float32)
-
-    def multiply(z, fresh=False):
-        def tile(n, _):
-            cols, value = product(z, n)
-            acc[:, cols] = value if fresh else acc[:, cols] + value
-            return 0
-
-        lax.fori_loop(0, QC // 256, tile, 0)
-
-    multiply(me.z, True)
+    multiply(three)
     for copy in sq_swap:
         copy.wait_recv()
     for n in range(2):
         sq_sum[n] = squares[2 * n + c] + sq_half[n]
     sq_far = remote(sq_sum.at[1 - me.yh], sq_full, sq_s.at[2], sq_g.at[2], far)
     sq_far.start()
-    multiply(me.zm)
-    multiply(me.zp)
     q_ring.last()
 
     def half_copy(n):
@@ -437,7 +450,7 @@
         return pl.ds(pl.multiple_of(p * TOK, TOK), TOK)
 
     def last_tile(n):
-        cols, value = product(me.z2, n)
+        cols, value = product(four, n)
         acc[:, cols] += value
         for m in range(2):
             half_sent[n, m] = acc[block(2 * m + 1 - c), cols].astype(jnp.bfloat16)
@@ -456,6 +469,7 @@
 
     for n in range(QC // 256):
         join_half(n)
+    w_ring.pass_on(0, 4)
     sq_far.wait_recv()
     mean = jnp.sum(sq_sum[me.yh] + sq_full[...], axis=1, keepdims=True) * (1.0 / D)
     gain = lax.rsqrt(mean + EPS)
@@ -497,7 +511,7 @@
         c_first(h, c_down.at[h], left).start()
         c_first(h, c_core.at[h], other).start()
         c_here[h].start()
-    w_ring.pass_on(0, 8)
+    w_ring.pass_on(4, 8)
     for h in range(2):
         c_along(xl, c, h, c_up.at[0], right).wait_recv()
         if h == 0:
@@ -507,32 +521,50 @@
         if h == 1:
             c_along(xr, c, h, c_down.at[2], left).start()
         c_along(xr, c, h, c_core.at[4 + h], other).start()
+
+    def from_other(x):
+        for h in range(2):
+            c_along(x, 1 - c, h, c_up.at[0], right).wait_recv()
+
+    def y_copy(j):
+        return remote(give.at[j], taken.at[j], y_s.at[j], y_g.at[j], near)
+
+    def term(j, n, fresh=False):
+        ws = obuf[(me.z + j) % 4, :, n].reshape(256, OC)
+        xs = ctx[n].reshape(2 * TOK, OC)
+        value = lax.dot_general(
+            xs, ws, (((1,), (1,)), ((), ())), preferred_element_type=jnp.float32
+        )
+        o_acc[j] = value if fresh else o_acc[j] + value
+
+    def terms(n, fresh=False):
+        def some(m, _):
+            term((m + 3) % 4, n, fresh)
+            return 0
+
+        lax.fori_loop(0, 3, some, 0)
+
+    def hand_over(j):
+        keep[j] = o_acc[j, :, pl.ds(pl.multiple_of(me.yl * 128, 128), 128)]
+        theirs = o_acc[j, :, pl.ds(pl.multiple_of((1 - me.yl) * 128, 128), 128)]
+        give[j] = theirs.astype(jnp.bfloat16)
+        y_copy(j).start()
+
+    for copy in c_here:
+        copy.wait()
+    from_other(me.x)
+    terms(me.x, True)
+    from_other(xl)
+    terms(xl)
+    from_other(xr)
+    terms(xr)
     for h in range(2):
         c_along(x2, c, h, c_up.at[0], right).wait_recv()
         c_along(x2, c, h, c_core.at[6 + h], other).start()
-    for x in (me.x, xl, xr, x2):
-        for h in range(2):
-            c_along(x, 1 - c, h, c_up.at[0], right).wait_recv()
-    for copy in c_here:
-        copy.wait()
-
-    def y_copy(j):
-        return remote(give.at[j], taken.at[j], y_s.at[j], y_g.at[j], near)
-
-    def features(j, z):
-        def term(n, _):
-            ws = obuf[z, :, n].reshape(256, OC)
-            xs = ctx[n].reshape(2 * TOK, OC)
-            value = lax.dot_general(
-                xs, ws, (((1,), (1,)), ((), ())), preferred_element_type=jnp.float32
-            )
-            o_acc[...] = jnp.where(n == 0, value, o_acc[...] + value)
-            return 0
-
-        lax.fori_loop(0, 4, term, 0)
-        keep[j] = o_acc[:, pl.ds(pl.multiple_of(me.yl * 128, 128), 128)]
-        give[j] = o_acc[:, pl.ds(pl.multiple_of((1 - me.yl) * 128, 128), 128)].astype(jnp.bfloat16)
-        y_copy(j).start()
+    from_other(x2)
+    for j in (0, 1, 3):
+        term(j, x2)
+        hand_over(j)
 
     def e_copy(j, z, m):
         core = (c + m) % 2
@@ -556,15 +588,18 @@
             here.start()
             here.wait()
 
-    features(0, me.z)
-    features(1, me.zm)
-    spread(0, me.z)
-    features(2, me.zp)
-    spread(1, me.zm)
     w_ring.last()
-    features(3, me.z2)
-    spread(2, me.zp)
-    spread(3, me.z2)
+    term(2, 0, True)
+
+    def rest(n, _):
+        term(2, n)
+        return 0
+
+    lax.fori_loop(1, 4, rest, 0)
+    hand_over(2)
+    places = [(me.z + j) % 4 for j in range(4)]
+    for j in (0, 1, 3, 2):
+        spread(j, places[j])
 
     @pl.when(jnp.logical_not(stays))
     def _():
@@ -599,7 +634,7 @@
         c_along(me.x, c, 0, c_down.at[n], left).wait_send()
     for n in range(8):
         c_along(me.x, c, 0, c_core.at[n], other).wait_send()
-    for j, z in enumerate((me.z, me.zm, me.zp, me.z2)):
+    for j, z in enumerate(places):
         y_copy(j).wait_send()
         e_copy(j, z, 1).wait_send()
 
@@ -659,7 +694,7 @@
             vmem(f32, PER_GROUP, TOK, HD),
             vmem(bf16, TOK, OC),
             vmem(bf16, 4, 2, 2, 128, OC),
-            vmem(f32, 2 * TOK, 256),
+            vmem(f32, 4, 2 * TOK, 256),
             vmem(f32, 4, 2 * TOK, 128),
             vmem(bf16, 4, 2 * TOK, 128),
             vmem(bf16, 4, 2 * TOK, 128),

time: 164 us -> 161 us (0.982)
  Pallas kernels: 160 us -> 157 us
    pallas_call x1, Pallas kernels: 160 us -> 157 us  [layer(): pl.pallas_call(layer_kernel, out_shape=jax.ShapeDtypeStruct((TOK, OC), bf...]
where the time goes in v3:
time: 161 us
  Pallas kernels  157 us (98%)
  local copies, waits for them, and re-layouts  3.99 us (2%)
    pallas_call x1, Pallas kernels, layer(): pl.pallas_call(layer_kernel, out_shape=jax.ShapeDtypeStruct((TOK, OC), bf...  157 us

profile of v3, /device:TPU:12, one launch (start us, length us, event | category | flops | bytes accessed | tf_op | source)
XLA Modules:
  0.0 161.3 jit_solution(9098008208248767423)
XLA Ops:
  0.0 2.0 %reshape.9.tok = bf16[256,1024]{1,0:T(8,128)(2,1)} reshape(bf16[64,4,1024]{2,1,0:T(4,128)(2,1)} %param.7) | data formatting | bytes 1048576 | tf_op jit(solution)/shard_map/reshape | solution.py:725
  2.0 157.3 %layer.1 = bf16[256,1024]{1,0:T(8,128)(2,1)} custom-call(s32[1,64]{1,0:T(1,128)} %row_pages.1, s32[1,64]{1,0:T(1,128)} %last_fill.1, s32[1,128]{1,0:T(1,128)} %order.1, bf16[256,1024]{1,0:T(8,128)(2,1)} %reshape.9.tok, bf16[64,10240]{1,0:T(8,128)(2,1)} %w_qkv.1, bf16[64,8192]{1,0:T(8,128)(2,1)} %w_out.1, bf16[128,256,128]{2,1,0:T(8,128)(2,1)} %bitcast.1), custom_call_target="tpu_custom_call" | custom-call | flops 9663676416 | bytes 16777216 | tf_op jit(solution)/shard_map/layer/pallas_call | solution.py:667
  159.2 2.0 %reshape.11 = bf16[64,4,1024]{2,1,0:T(4,128)(2,1)} reshape(bf16[256,1024]{1,0:T(8,128)(2,1)} %layer.1) | data formatting | bytes 1048576 | tf_op jit(solution)/shard_map/reshape | solution.py:727

commit v4 on v3

--- a/solution.py
+++ b/solution.py
@@ -229,12 +229,12 @@
 
         lax.fori_loop(low, high, two, 0)
 
-    def last(self):
+    def last(self, low, high):
         def one(k, _):
             self.arrived(self.me.z2, self.order(k))
             return 0
 
-        lax.fori_loop(0, self.count, one, 0)
+        lax.fori_loop(low, high, one, 0)
 
     def finish(self):
         def one(k, _):
@@ -260,7 +260,7 @@
     mine, ctx, o_acc, keep, give, taken, sums, final,
     own_sem, cache_sem,
     q_sent, q_up, q_down, q_got,
-    w_sent, w_up, w_down, w_got,
+    w_sent, w_up, w_down, w_got, v_sent,
     x_sent, x_up, x_down, x_got,
     sq_s, sq_g, h_s, h_g, f_s, f_g,
     c_up, c_down, c_core, c_got,
@@ -354,9 +354,28 @@
         return obuf.at[z, p // 4, p % 4]
 
     def w_plane(k):
-        y, n = (me.y + k // 4) % 4, k % 4
+        y = jnp.where(k == 4, me.yh * 2 + 1 - me.yl, (me.y + 1 + (k - 5) // 3) % 4)
+        n = jnp.where(k == 4, 3, (k - 5) % 3)
         p = me.y * 4 + n
         return remote(w_columns(y % 2, n), w_slot(me.z, p), w_sent.at[k], w_got.at[me.z, p], me.at(y=y))
+
+    def w_order(k):
+        first = me.y * 4 + (k + 3) % 4
+        later = ((me.y + 3 - (k - 5) // 3) % 4) * 4 + (k - 5) % 3
+        swap = (me.yh * 2 + 1 - me.yl) * 4 + 3
+        return jnp.where(k < 4, first, jnp.where(k == 4, swap, later))
+
+    def w_far(j, m):
+        z, p = (me.z + j) % 4, (me.yh * 2 + m) * 4 + 3
+        return remote(w_slot(z, p), w_slot(z, p), v_sent.at[j, m], w_got.at[z, p], far)
+
+    def w_cross(j):
+        for m in range(2):
+            w_far(j, m).start()
+
+    def w_crossed(j):
+        for m in range(2):
+            w_ring.arrived((me.z + j) % 4, ((1 - me.yh) * 2 + m) * 4 + 3)
 
     def w_start(k, _):
         w_plane(k).start()
@@ -364,13 +383,13 @@
 
     w_here = [
         pltpu.make_async_copy(w_columns(me.yl, n), w_slot(me.z, me.y * 4 + n), own_sem.at[2 + n])
-        for n in range(4)
+        for n in (3, 0, 1, 2)
     ]
     for copy in w_here:
         copy.start()
-    lax.fori_loop(4, 16, w_start, 0)
+    lax.fori_loop(4, 14, w_start, 0)
     w_ring = Ring(
-        me, 16, lambda k: ((me.y + 4 - k // 4) % 4) * 4 + k % 4, w_slot, w_up, w_down, w_got
+        me, 14, w_order, w_slot, w_up, w_down, w_got
     )
 
 
@@ -398,6 +417,7 @@
     q_ring.pass_on(0, 4)
     w_ring.pass_local(w_here)
     w_ring.pass_own(4)
+    w_cross(0)
 
     def product(z, n):
         cols = pl.ds(pl.multiple_of(n * 256, 256), 256)
@@ -438,7 +458,7 @@
         sq_sum[n] = squares[2 * n + c] + sq_half[n]
     sq_far = remote(sq_sum.at[1 - me.yh], sq_full, sq_s.at[2], sq_g.at[2], far)
     sq_far.start()
-    q_ring.last()
+    q_ring.last(0, TP)
 
     def half_copy(n):
         return remote(half_sent.at[n], half_got.at[n], h_s.at[n], h_g.at[n], other)
@@ -470,6 +490,8 @@
     for n in range(QC // 256):
         join_half(n)
     w_ring.pass_on(0, 4)
+    w_cross(1)
+    w_cross(3)
     sq_far.wait_recv()
     mean = jnp.sum(sq_sum[me.yh] + sq_full[...], axis=1, keepdims=True) * (1.0 / D)
     gain = lax.rsqrt(mean + EPS)
@@ -511,7 +533,10 @@
         c_first(h, c_down.at[h], left).start()
         c_first(h, c_core.at[h], other).start()
         c_here[h].start()
-    w_ring.pass_on(4, 8)
+    w_ring.pass_on(4, 7)
+    w_ring.arrived(me.z2, w_order(0))
+    w_ring.arrived(me.z2, w_order(4))
+    w_cross(2)
     for h in range(2):
         c_along(xl, c, h, c_up.at[0], right).wait_recv()
         if h == 0:
@@ -553,6 +578,8 @@
     for copy in c_here:
         copy.wait()
     from_other(me.x)
+    for j in (0, 1, 3):
+        w_crossed(j)
     terms(me.x, True)
     from_other(xl)
     terms(xl)
@@ -588,7 +615,9 @@
             here.start()
             here.wait()
 
-    w_ring.last()
+    w_ring.last(1, 4)
+    w_ring.last(5, 14)
+    w_crossed(2)
     term(2, 0, True)
 
     def rest(n, _):
@@ -620,7 +649,10 @@
         return 0
 
     lax.fori_loop(1, TP, q_done, 0)
-    lax.fori_loop(4, 16, w_done, 0)
+    lax.fori_loop(4, 14, w_done, 0)
+    for j in range(4):
+        for m in range(2):
+            w_far(j, m).wait_send()
     q_ring.finish()
     w_ring.finish()
     for copy in sq_swap:
@@ -704,7 +736,7 @@
             dma((8,)),
         ]
         + ring_sems(TP)
-        + ring_sems(16)
+        + [dma((14,)), dma((21,)), dma((21,)), dma((4, 16)), dma((4, 2))]
         + [dma((4,)), dma((6,)), dma((6,)), dma((4, 4))]
         + [dma((3,)), dma((3,)), dma((tiles,)), dma((tiles,)), dma((tiles,)), dma((tiles,))]
         + [dma((3,)), dma((3,)), dma((8,)), dma((4, 2, 2))]

time: 161 us -> 161 us (level); the launches traced: 161 us -> 159 us
  Pallas kernels: 157 us -> 155 us
    pallas_call x1, Pallas kernels: 157 us -> 155 us  [layer(): pl.pallas_call(layer_kernel, out_shape=jax.ShapeDtypeStruct((TOK, OC), bf...]
where the time goes in v4:
time: 161 us; the launch traced here: 159 us
  Pallas kernels  155 us (96%)
  local copies, waits for them, and re-layouts  3.99 us (2%)
    pallas_call x1, Pallas kernels, layer(): pl.pallas_call(layer_kernel, out_shape=jax.ShapeDtypeStruct((TOK, OC), bf...  155 us

profile of v4, /device:TPU:12, one launch (start us, length us, event | category | flops | bytes accessed | tf_op | source)
XLA Modules:
  0.0 159.2 jit_solution(5084068691991586863)
XLA Ops:
  0.0 2.0 %reshape.9.tok = bf16[256,1024]{1,0:T(8,128)(2,1)} reshape(bf16[64,4,1024]{2,1,0:T(4,128)(2,1)} %param.7) | data formatting | bytes 1048576 | tf_op jit(solution)/shard_map/reshape | solution.py:757
  2.0 155.2 %layer.1 = bf16[256,1024]{1,0:T(8,128)(2,1)} custom-call(s32[1,64]{1,0:T(1,128)} %row_pages.1, s32[1,64]{1,0:T(1,128)} %last_fill.1, s32[1,128]{1,0:T(1,128)} %order.1, bf16[256,1024]{1,0:T(8,128)(2,1)} %reshape.9.tok, bf16[64,10240]{1,0:T(8,128)(2,1)} %w_qkv.1, bf16[64,8192]{1,0:T(8,128)(2,1)} %w_out.1, bf16[128,256,128]{2,1,0:T(8,128)(2,1)} %bitcast.1), custom_call_target="tpu_custom_call" | custom-call | flops 9663676416 | bytes 16777216 | tf_op jit(solution)/shard_map/layer/pallas_call | solution.py:699
  157.1 2.0 %reshape.11 = bf16[64,4,1024]{2,1,0:T(4,128)(2,1)} reshape(bf16[256,1024]{1,0:T(8,128)(2,1)} %layer.1) | data formatting | bytes 1048576 | tf_op jit(solution)/shard_map/reshape | solution.py:759

commit v5 on v4

--- a/solution.py
+++ b/solution.py
@@ -615,6 +615,9 @@
             here.start()
             here.wait()
 
+    places = [(me.z + j) % 4 for j in range(4)]
+    for j in (0, 1, 3):
+        spread(j, places[j])
     w_ring.last(1, 4)
     w_ring.last(5, 14)
     w_crossed(2)
@@ -626,8 +629,7 @@
 
     lax.fori_loop(1, 4, rest, 0)
     hand_over(2)
-    places = [(me.z + j) % 4 for j in range(4)]
-    for j in (0, 1, 3, 2):
+    for j in (2,):
         spread(j, places[j])
 
     @pl.when(jnp.logical_not(stays))

time: 161 us -> 165 us (1.025)
  Pallas kernels: 155 us -> 159 us
    pallas_call x1, Pallas kernels: 155 us -> 159 us  [layer(): pl.pallas_call(layer_kernel, out_shape=jax.ShapeDtypeStruct((TOK, OC), bf...]
where the time goes in v5:
time: 165 us; the launch traced here: 163 us
  Pallas kernels  159 us (96%)
  local copies, waits for them, and re-layouts  3.99 us (2%)
    pallas_call x1, Pallas kernels, layer(): pl.pallas_call(layer_kernel, out_shape=jax.ShapeDtypeStruct((TOK, OC), bf...  159 us

profile of v5, /device:TPU:12, one launch (start us, length us, event | category | flops | bytes accessed | tf_op | source)
XLA Modules:
  0.0 162.5 jit_solution(2377840770631977360)
XLA Ops:
  0.0 2.0 %reshape.9.tok = bf16[256,1024]{1,0:T(8,128)(2,1)} reshape(bf16[64,4,1024]{2,1,0:T(4,128)(2,1)} %param.7) | data formatting | bytes 1048576 | tf_op jit(solution)/shard_map/reshape | solution.py:759
  2.0 158.5 %layer.1 = bf16[256,1024]{1,0:T(8,128)(2,1)} custom-call(s32[1,64]{1,0:T(1,128)} %row_pages.1, s32[1,64]{1,0:T(1,128)} %last_fill.1, s32[1,128]{1,0:T(1,128)} %order.1, bf16[256,1024]{1,0:T(8,128)(2,1)} %reshape.9.tok, bf16[64,10240]{1,0:T(8,128)(2,1)} %w_qkv.1, bf16[64,8192]{1,0:T(8,128)(2,1)} %w_out.1, bf16[128,256,128]{2,1,0:T(8,128)(2,1)} %bitcast.1), custom_call_target="tpu_custom_call" | custom-call | flops 9663676416 | bytes 16777216 | tf_op jit(solution)/shard_map/layer/pallas_call | solution.py:701
  160.5 2.0 %reshape.11 = bf16[64,4,1024]{2,1,0:T(4,128)(2,1)} reshape(bf16[256,1024]{1,0:T(8,128)(2,1)} %layer.1) | data formatting | bytes 1048576 | tf_op jit(solution)/shard_map/reshape | solution.py:761
